TPU v7x, 32 devices: a whole 2x2x4 slice. The times are simulated.
32 devices in a mesh: dom: 16 (over z, y, core), rep: 2 (over x).
Axes of the slice: x: 2, y: 2, z: 4, core: 2. Of those that a mesh axis runs over, the one named last changes fastest.
Arguments:
- features: bfloat16 [8192, 768], P('dom'), may hold values from -6 to 6
- tiles: bfloat16 [64, 16, 4, 128, 128], P('dom', 'rep'), may hold values from -0.0625 to 0.0625
- tile_cols: int32 [64, 16, 4], P('dom', 'rep'), may hold values from 0 to 3
- tile_mask: int32 [64, 16, 4], P('dom', 'rep'), may hold values from 0 to 1, as said below
- weight: bfloat16 [768, 768], replicated, may hold values from -0.21875 to 0.21875
- bias: float32 [768], replicated, may hold values from -3 to 3
- cotangent: bfloat16 [8192, 768], P(('dom', 'rep')), may hold values from -0.06591797 to 0.06591797
Outputs:
- output: bfloat16 [8192, 768], P(('dom', 'rep'))
- grad_weight: float32 [768, 768], replicated
- grad_bias: float32 [768], replicated
Inputs may be any that keep to these rules, and one draw needn't show every extreme that they name: `tile_mask`: for each row block and source, the live slots come first and slot 0 is always live.
All inputs are finite; a program needn't handle non-finite values.
Results may differ from a plain program's by a relative error of at most 0.02.
Values may be sent and summed in bfloat16 or wider, within the bound.
A program may use at most 128 MiB of HBM per device.

v0:
```python
import jax
import jax.numpy as jnp
from jax import lax
from jax.sharding import PartitionSpec as P


def spread(value, axis, source):
    kept = jnp.where(lax.axis_index(axis) == source, value, 0).astype(value.dtype)
    return lax.psum(kept, axis)


def section_term(source, tiles, tile_cols, tile_mask, section):
    rblocks = tiles.shape[0]
    tile_side = tiles.shape[3]
    feat_width = source.shape[1]
    source_blocks = source.reshape(source.shape[0] // tile_side, tile_side, feat_width)
    columns = lax.dynamic_index_in_dim(tile_cols, section, 1, keepdims=False)
    live = lax.dynamic_index_in_dim(tile_mask, section, 1, keepdims=False)
    tile_set = lax.dynamic_index_in_dim(tiles, section, 1, keepdims=False)
    block_ids = jnp.arange(source_blocks.shape[0])
    selector = ((columns[:, :, None] == block_ids[None, None, :]) * live[:, :, None]).astype(
        jnp.bfloat16
    )
    picked = jnp.einsum(
        "bkc,cjd->bkjd", selector, source_blocks, preferred_element_type=jnp.float32
    ).astype(jnp.bfloat16)
    summed = jnp.einsum("bkij,bkjd->bid", tile_set, picked, preferred_element_type=jnp.float32)
    return summed.reshape(rblocks * tile_side, feat_width)


def on_device(features, tiles, tile_cols, tile_mask, weight, bias, cotangent):
    sections = tiles.shape[1]
    replica = lax.axis_index("rep")
    aggregate = jnp.zeros(features.shape, jnp.float32)
    for turn_index in range(sections):
        root_index = replica * sections + turn_index
        source = spread(features, "dom", root_index)
        aggregate = aggregate + section_term(source, tiles, tile_cols, tile_mask, turn_index)
    rows_sum = lax.psum_scatter(
        aggregate.astype(jnp.bfloat16), "rep", scatter_dimension=0, tiled=True
    )
    pre_act = jnp.dot(rows_sum, weight, preferred_element_type=jnp.float32) + bias
    sigmoid_pre = jax.nn.sigmoid(pre_act)
    output = (pre_act * sigmoid_pre).astype(jnp.bfloat16)
    grad_pre = cotangent.astype(jnp.float32) * sigmoid_pre * (1.0 + pre_act * (1.0 - sigmoid_pre))
    grad_low = grad_pre.astype(jnp.bfloat16)
    local_weight = jnp.einsum("nd,ne->de", rows_sum, grad_low, preferred_element_type=jnp.float32)
    local_bias = jnp.sum(grad_pre, axis=0)
    grad_weight, grad_bias = lax.psum((local_weight, local_bias), ("dom", "rep"))
    return (output, grad_weight, grad_bias)


def solution(mesh):
    placed = (
        P("dom", None),
        P("dom", "rep", None, None, None),
        P("dom", "rep", None),
        P("dom", "rep", None),
        P(),
        P(),
        P(("dom", "rep"), None),
    )
    return jax.shard_map(
        on_device,
        mesh=mesh,
        in_specs=placed,
        out_specs=(P(("dom", "rep"), None), P(), P()),
        check_vma=False,
    )
```

profile of v0, /device:TPU:0, one launch (start us, length us, event | category | flops | bytes accessed | tf_op | source)
XLA Modules:
  0.0 354.4 jit_solution(4255617056603301633)
XLA Ops:
  7.2 4.0 %broadcast_select_fusion = (bf16[512,768]{1,0:T(8,128)(2,1)}, bf16[512,768]{1,0:T(8,128)(2,1)}, bf16[512,768]{1,0:T(8,128)(2,1)}, bf16[512,768]{1,0:T(8,128)(2,1...) fusion(bf16[512,768]{1,0:T(8,128)(2,1)} %param.7, ...), kind=kLoop, calls=%fused_computation.44 | loop fusion | flops 3145728 | bytes 7077896 | tf_op jit(solution)/shard_map/jit(_where)/select_n | solution.py:8
  13.2 144.5 %all-reduce.6.cloned.1.call-done = (bf16[4,128,768]{2,1,0:T(8,128)(2,1)}, bf16[4,128,768]{2,1,0:T(8,128)(2,1)}, bf16[4,128,768]{2,1,0:T(8,128)(2,1)}, bf16[4,128...) async-done(((bf16[4,128,768]{2,1,0:T(8,128)(2,1)}, ...) | async-done | bytes 6291472 | tf_op jit(solution)/shard_map/psum | solution.py:9
  157.7 2.5 fusion.13
  160.2 1.7 fusion.5
  161.9 1.4 fusion.11
  163.3 1.7 fusion.6
  165.0 1.4 fusion.15
  166.4 1.7 fusion.4
  168.2 1.4 fusion.17
  169.6 1.7 fusion.3
  171.3 1.4 fusion.19
  172.7 1.7 fusion.2
  174.4 1.4 fusion.21
  175.8 1.9 fusion.1
  177.8 1.4 fusion.23
  179.1 1.7 fusion
  180.9 1.4 fusion.9
  182.3 3.1 fusion.8
  185.4 17.6 %reduce-scatter.2.cloned.1.call-done = bf16[256,768]{1,0:T(8,128)(2,1)} async-done(((bf16[512,768]{1,0:T(8,128)(2,1)}), bf16[256,768]{1,0:T(8,128)(2,1)}) %reduce-scatter.2.cloned.1.call-update) | async-done | bytes 393232 | tf_op jit(solution)/shard_map/reduce_scatter | solution.py:39
  203.0 2.5 fusion.91
  205.5 2.1 fusion.41
  207.7 39.6 %psum.79 = f32[768]{0:T(1024)} all-reduce(f32[768]{0:T(1024)S(1)} %get-tuple-element.27), channel_id=1, replica_groups=mesh['dom'=16,'rep'=2] {'dom','rep'}, use_global_device_ids=true, to_apply=%region_11.12 | all-reduce | flops 768 | bytes 6144 | tf_op jit(solution)/shard_map/psum | solution.py:49
  247.3 97.3 %all-reduce.4.cloned.1.call-done = f32[768,768]{1,0:T(8,128)} async-done(((f32[768,768]{1,0:T(8,128)}), f32[768,768]{1,0:T(8,128)}) %all-reduce.4.cloned.1.call-update) | async-done | bytes 2359312 | tf_op jit(solution)/shard_map/psum | solution.py:49
  344.6 3.2 copy.109
  (33 shorter events, 2.1 us)
Async XLA Ops:
  7.2 195.9 %copy-start = (bf16[768,768]{1,0:T(8,128)(2,1)S(1)}, bf16[768,768]{1,0:T(8,128)(2,1)}, u32[]{:S(2)}) copy-start(bf16[768,768]{1,0:T(8,128)(2,1)} %param.11) | copy-start | bytes 3538948
  7.2 150.5 %all-reduce.6.cloned.1.call-start = ((), (), s32[]{:S(2)}) async-start(), calls=%async_computation.3 | async-start | bytes 12582912 | tf_op jit(solution)/shard_map/psum | solution.py:9
  11.2 0.7 copy-start.8
  11.2 0.7 copy-start.9
  11.2 191.8 %reduce-scatter.2.cloned.1.call-start = ((), (), s32[]{:S(2)}) async-start(), calls=%async_computation.1 | async-start | bytes 1179648 | tf_op jit(solution)/shard_map/reduce_scatter | solution.py:39
  160.2 1.7 copy-start.7
  163.3 1.7 copy-start.6
  166.4 1.7 copy-start.5
  169.5 1.7 copy-start.4
  172.7 1.7 copy-start.3
  175.8 2.0 copy-start.2
  179.1 1.7 copy-start.1
  182.2 20.8 %copy-start.10 = (bf16[256,768]{1,0:T(8,128)(2,1)S(1)}, bf16[256,768]{1,0:T(8,128)(2,1)}, u32[]{:S(2)}) copy-start(bf16[256,768]{1,0:T(8,128)(2,1)} %param.13) | copy-start | bytes 1179652
  182.3 20.8 %copy-start.12 = (f32[768]{0:T(1024)S(1)}, f32[768]{0:T(1024)}, u32[]{:S(2)}) copy-start(f32[768]{0:T(1024)} %param.12) | copy-start | bytes 9220
  185.4 159.2 %all-reduce.4.cloned.1.call-start = ((), (), s32[]{:S(2)}) async-start(), calls=%async_computation.2 | async-start | bytes 4718592 | tf_op jit(solution)/shard_map/psum | solution.py:49
  203.0 2.5 copy-start.11
Sparse Core Ops, SparseCore 0:
  13.1 144.4 all-reduce.5
  185.5 17.4 reduce-scatter.1
  209.1 135.4 all-reduce.3
where the time goes:
time: 355 us; the launch traced here: 354 us
  waiting for transfers between devices  259 us (73%)
  blocking collectives  39.6 us (11%)
  matrix products  32 us (9%)
  between operations  14 us (4%)
  local copies, waits for them, and re-layouts  5.18 us (1%)
  other arithmetic  3.97 us (1%)
    psum x1, waiting for transfers between devices, spread(): return lax.psum(kept, axis)  144 us
    psum x1, waiting for transfers between devices, on_device(): lax.psum((local_weight, local_bias), ('dom', 'rep'))  97.3 us
    psum x1, blocking collectives, on_device(): lax.psum((local_weight, local_bias), ('dom', 'rep'))  39.6 us
    reduce_scatter x1, waiting for transfers between devices, on_device(): lax.psum_scatter(aggregate.astype(jnp.bfloat16), 'rep', scatter_dimension...  17.6 us
    dot_general x8, matrix products, section_term(): jnp.einsum('bkij,bkjd->bid', tile_set, picked, preferred_element_type=jnp...  15.3 us
    dot_general x8, matrix products, section_term(): jnp.einsum('bkc,cjd->bkjd', selector, source_blocks, preferred_element_ty...  12.1 us
  transfers between devices with their start and end apart: 3, of which 3 were waited for; matrix products, arithmetic and copies ran while one was open for 0% of the time, Pallas kernels for 0%

commit v1 on v0

--- a/solution.py
+++ b/solution.py
@@ -1,7 +1,16 @@
+import functools
+
 import jax
 import jax.numpy as jnp
 from jax import lax
+from jax.experimental import pallas as pl
+from jax.experimental.pallas import tpu as pltpu
 from jax.sharding import PartitionSpec as P
+
+MESH = pl.DeviceIdType.MESH
+CHUNKS = 8
+F32 = jnp.float32
+BF16 = jnp.bfloat16
 
 
 def spread(value, axis, source):
@@ -50,6 +59,402 @@
     return (output, grad_weight, grad_bias)
 
 
+ORDERS = (("x", "y", "z"), ("y", "z", "x"), ("z", "x", "y"))
+WAYS = {"x": 2, "y": 2, "z": 4}
+
+
+def part_rows(group_rows, order, stage):
+    rows = group_rows
+    for axis in order[: stage + 1]:
+        rows //= WAYS[axis]
+    return rows
+
+
+def kernel(feat_hbm, tiles_hbm, cols, mask, weight_hbm, bias_ref, cot_hbm,
+           out_ref, gw_ref, gb_ref,
+           s000, s001, s010, s011, s100, s101, s110, s111,
+           tiles_v, weight_v, cot_v, dense, acc,
+           part_out, part_in, mixed, glow,
+           gacc, gsend, gcore_in, gfin, gother, gfull_in,
+           rb00, rb01, rb02, rb10, rb11, rb12, rb20, rb21, rb22,
+           bstate, brecv,
+           lsem, zrecv, yrecv, crecv, zup, zdown, ysend, csend,
+           psend, precv, gcs, gcr, rs_s, rs_r, ag_s, ag_r, fs, fr, bs, br):
+    slots = [[[s000, s001], [s010, s011]], [[s100, s101], [s110, s111]]]
+    rbufs = [[rb00, rb01, rb02], [rb10, rb11, rb12], [rb20, rb21, rb22]]
+    me = lax.axis_index("dom")
+    r = lax.axis_index("rep")
+    z = lax.div(me, 4)
+    y = lax.rem(lax.div(me, 2), 2)
+    c = lax.rem(me, 2)
+    w = z + r * (3 - 2 * z)
+    dz = 1 - 2 * r
+    rblocks, sections, ways, side, _ = tiles_v.shape
+    rows, width = acc.shape
+    crows = rows // CHUNKS
+    half = rows // 2
+
+    def dev(zz, yy, cc, rr):
+        return (zz * 4 + yy * 2 + cc, rr)
+
+    def z_peer(d):
+        z2 = lax.rem(lax.div(z, 2) + d // 2, 2)
+        z1 = lax.rem(lax.rem(z, 2) + d % 2, 2)
+        return z2 * 2 + z1
+
+    peers = {
+        "x": [dev(z, y, c, 1 - r)],
+        "y": [dev(z, 1 - y, c, r)],
+        "z": [dev(z_peer(d), y, c, r) for d in (1, 2, 3)],
+    }
+    places = {"x": [1 - r], "y": [1 - y], "z": [z_peer(d) for d in (1, 2, 3)]}
+    mine = {"x": r, "y": y, "z": z}
+    other_core = dev(z, y, 1 - c, r)
+    up = dev(jnp.clip(z + dz, 0, 3), y, c, r)
+    down = dev(jnp.clip(z - dz, 0, 3), y, c, r)
+
+    def remote(src, dst, ss, rs, device):
+        return pltpu.make_async_remote_copy(
+            src_ref=src, dst_ref=dst, send_sem=ss, recv_sem=rs, device_id=device, device_id_type=MESH
+        )
+
+    for i in range(2):
+        @pl.when(w == i)
+        def _():
+            pltpu.make_async_copy(feat_hbm, slots[i][0][0], lsem.at[0]).start()
+    tiles_load = pltpu.make_async_copy(tiles_hbm, tiles_v, lsem.at[1])
+    weight_load = pltpu.make_async_copy(weight_hbm, weight_v, lsem.at[2])
+    cot_load = pltpu.make_async_copy(cot_hbm, cot_v, lsem.at[3])
+    tiles_load.start()
+    weight_load.start()
+    cot_load.start()
+    barrier = pltpu.get_barrier_semaphore()
+    greeted = [other_core] + peers["x"] + peers["y"] + peers["z"]
+    for device in greeted:
+        pl.semaphore_signal(barrier, inc=1, device_id=device, device_id_type=MESH)
+    pl.semaphore_wait(barrier, len(greeted))
+
+    def chunk(ch):
+        return pl.ds(pl.multiple_of(ch * crows, crows), crows)
+
+    def z_copy(i, at, sem, rsem, device):
+        slot = slots[i][0][0]
+        return remote(slot.at[at], slot.at[at], sem, rsem, device)
+
+    def y_copy(i, at, rsem):
+        return remote(slots[i][0][0].at[at], slots[i][1][0].at[at], ysend.at[i], rsem, peers["y"][0])
+
+    def c_copy(i, j, at):
+        return remote(slots[i][j][0].at[at], slots[i][j][1].at[at],
+                      csend.at[2 * i + j], crecv.at[2 * i + j], other_core)
+
+    everything = pl.ds(0, rows)
+    ups = {0: w <= 2, 1: jnp.logical_and(w >= 1, w <= 2)}
+
+    def forward(i, ch):
+        at = chunk(ch)
+
+        @pl.when(ups[i])
+        def _():
+            z_copy(i, at, zup.at[i], zrecv.at[i, ch], up).start()
+
+        if i == 1:
+            @pl.when(w == 1)
+            def _():
+                z_copy(i, at, zdown.at[0], zrecv.at[i, ch], down).start()
+        y_copy(i, at, yrecv.at[i, ch]).start()
+        c_copy(i, 0, at).start()
+
+    def z_step(i, ch):
+        @pl.when(w != i)
+        def _():
+            z_copy(i, chunk(ch), zup.at[i], zrecv.at[i, ch], up).wait_recv()
+            forward(i, ch)
+
+    def y_step(i, ch):
+        y_copy(i, chunk(ch), yrecv.at[i, ch]).wait_recv()
+        c_copy(i, 1, chunk(ch)).start()
+
+    for i in range(2):
+        @pl.when(w == i)
+        def _():
+            pltpu.make_async_copy(feat_hbm, slots[i][0][0], lsem.at[0]).wait()
+
+            @pl.loop(0, CHUNKS)
+            def _(ch):
+                forward(i, ch)
+    tiles_load.wait()
+
+    def assemble(index):
+        i = 1 - lax.div(index, 4)
+        j = lax.rem(lax.div(index, 2), 2)
+        k = lax.rem(index, 2)
+        zz = i + r * (1 - 2 * i)
+        section = zz * 4 + (y + j - 2 * y * j) * 2 + (c + k - 2 * c * k)
+
+        @pl.loop(0, rblocks)
+        def _(b):
+            base = (b * sections + section) * ways
+            tile_of = [tiles_v[b, section, t].astype(F32) for t in range(ways)]
+            for block in range(rows // side):
+                total = None
+                for t in range(ways):
+                    take = jnp.logical_and(cols[base + t] == block, mask[base + t] != 0)
+                    term = tile_of[t] * jnp.where(take, 1.0, 0.0)
+                    total = term if total is None else total + term
+                dense[index, pl.ds(pl.multiple_of(b * side, side), side),
+                      block * side:(block + 1) * side] = total.astype(BF16)
+
+    @pl.loop(0, CHUNKS)
+    def _(ch):
+        z_step(1, ch)
+
+        @pl.when(ch > 0)
+        def _():
+            y_step(1, ch - 1)
+        assemble(ch)
+
+    def product(i, j, k, at, lanes):
+        index = (1 - i) * 4 + j * 2 + k
+        return jnp.dot(dense[index, at, :], slots[i][j][k][:, lanes], preferred_element_type=F32)
+
+    z_step(0, 0)
+    y_step(1, CHUNKS - 1)
+    for step in range(1, CHUNKS):
+        z_step(0, step)
+        y_step(0, step - 1)
+        if step % 2 == 1:
+            j, k = step // 4, (step // 2) % 2
+            if k == 1:
+                c_copy(1, j, everything).wait_recv()
+
+            @pl.loop(0, width // 256)
+            def _(n):
+                lanes = pl.ds(pl.multiple_of(n * 256, 256), 256)
+                term = product(1, j, k, everything, lanes)
+                if step == 1:
+                    acc[:, lanes] = term
+                else:
+                    acc[:, lanes] = acc[:, lanes] + term
+    y_step(0, CHUNKS - 1)
+    c_copy(0, 0, everything).wait_recv()
+    c_copy(0, 1, everything).wait_recv()
+
+    def finish(start, target):
+        at = pl.ds(pl.multiple_of(start, half), half)
+
+        @pl.loop(0, width // 256)
+        def _(n):
+            lanes = pl.ds(pl.multiple_of(n * 256, 256), 256)
+            total = acc[at, lanes]
+            for j in range(2):
+                for k in range(2):
+                    total = total + product(0, j, k, at, lanes)
+            target[:, lanes] = total.astype(BF16)
+
+    def p_copy(t):
+        at = pl.ds(t * (half // 2), half // 2)
+        return remote(part_out.at[at], part_in.at[at], psend.at[t], precv.at[t], peers["x"][0])
+
+    finish((1 - r) * half, part_out)
+    for t in range(2):
+        p_copy(t).start()
+    finish(r * half, mixed)
+    weight_load.wait()
+    cot_load.wait()
+
+    bias_rows = jnp.zeros((8, width), F32)
+    for t in range(2):
+        at = slice(t * (half // 2), (t + 1) * (half // 2))
+        p_copy(t).wait_recv()
+        low = (mixed[at, :].astype(F32) + part_in[at, :].astype(F32)).astype(BF16)
+        mixed[at, :] = low
+        pre = jnp.dot(low, weight_v[...], preferred_element_type=F32) + bias_ref[...]
+        sig = 1.0 / (1.0 + jnp.exp(-pre))
+        out_ref[at, :] = (pre * sig).astype(BF16)
+        grad = cot_v[at, :].astype(F32) * sig * (1.0 + pre * (1.0 - sig))
+        glow[at, :] = grad.astype(BF16)
+        bias_rows = bias_rows + jnp.sum(grad.reshape(half // 16, 8, width), axis=0)
+
+    cw = width // 2
+
+    def grad_half(start):
+        lanes = pl.ds(pl.multiple_of(start, 128), cw)
+        return lax.dot_general(mixed[...], glow[:, lanes], (((0,), (0,)), ((), ())),
+                               preferred_element_type=F32)
+
+    def b_send(stage, axis_peers, first):
+        copies = []
+        for d, device in enumerate(axis_peers):
+            copies.append(remote(bstate.at[stage], brecv.at[first + d], bs.at[first + d],
+                                 br.at[first + d], device))
+            copies[-1].start()
+        return copies
+
+    def b_sum(stage, copies, first):
+        for copy in copies:
+            copy.wait_recv()
+        total = bstate[stage] + brecv[first]
+        if len(copies) == 3:
+            total = total + (brecv[first + 1] + brecv[first + 2])
+        bstate[stage + 1] = total
+
+    sent = []
+    bstate[0] = bias_rows
+    gsend_core = gother
+    gsend_core[...] = grad_half((1 - c) * cw).astype(BF16)
+    core_copy = remote(gsend_core, gcore_in, gcs, gcr, other_core)
+    core_copy.start()
+    b_copies = b_send(0, [other_core], 0)
+    gacc[...] = grad_half(c * cw)
+    core_copy.wait_recv()
+    gacc[...] = gacc[...] + gcore_in[...].astype(F32)
+    b_sum(0, b_copies, 0)
+    sent += [core_copy] + b_copies
+
+    group_rows = width // 3
+    starts = [g * group_rows for g in range(3)]
+    history = [[], [], []]
+    b_first = (1, 2, 3)
+    for stage in range(3):
+        flying = []
+        for g, order in enumerate(ORDERS):
+            axis = order[stage]
+            size = part_rows(group_rows, order, stage)
+            copies = []
+            for d, (device, place) in enumerate(zip(peers[axis], places[axis])):
+                at = pl.ds(pl.multiple_of(starts[g] + place * size, size), size)
+                gsend[at, :] = gacc[at, :].astype(BF16)
+                copy = remote(gsend.at[at], rbufs[g][stage].at[d],
+                              rs_s.at[g, stage, d], rs_r.at[g, stage, d], device)
+                copy.start()
+                copies.append(copy)
+            flying.append(copies)
+        b_copies = b_send(stage + 1, peers[ORDERS[0][stage]], b_first[stage])
+        for g, order in enumerate(ORDERS):
+            axis = order[stage]
+            size = part_rows(group_rows, order, stage)
+            for copy in flying[g]:
+                copy.wait_recv()
+            keep = starts[g] + mine[axis] * size
+            at = pl.ds(pl.multiple_of(keep, size), size)
+            total = gacc[at, :]
+            for d in range(len(flying[g])):
+                total = total + rbufs[g][stage][d].astype(F32)
+            gacc[at, :] = total
+            history[g].append(starts[g])
+            starts[g] = keep
+            sent += flying[g]
+        b_sum(stage + 1, b_copies, b_first[stage])
+        sent += b_copies
+    gb_ref[...] = jnp.sum(bstate[4], axis=0, keepdims=True)
+
+    last = part_rows(group_rows, ORDERS[0], 2)
+    for g in range(3):
+        at = pl.ds(pl.multiple_of(starts[g], last), last)
+        gfin[at, :] = gacc[at, :].astype(BF16)
+    for stage in (2, 1, 0):
+        flying = []
+        for g, order in enumerate(ORDERS):
+            axis = order[stage]
+            size = part_rows(group_rows, order, stage)
+            at = pl.ds(pl.multiple_of(starts[g], size), size)
+            for d, device in enumerate(peers[axis]):
+                copy = remote(gfin.at[at], gfin.at[at],
+                              ag_s.at[g, stage, d], ag_r.at[g, stage, d], device)
+                copy.start()
+                sent.append(copy)
+            for d, place in enumerate(places[axis]):
+                there = pl.ds(pl.multiple_of(history[g][stage] + place * size, size), size)
+                flying.append(remote(gfin.at[there], gfin.at[there],
+                                     ag_s.at[g, stage, d], ag_r.at[g, stage, d], peers[axis][d]))
+            starts[g] = history[g][stage]
+        for copy in flying:
+            copy.wait_recv()
+    core_copy.wait_send()
+    sent.remove(core_copy)
+    final = remote(gfin, gfull_in, fs, fr, other_core)
+    final.start()
+    gw_ref[:, pl.ds(pl.multiple_of(c * cw, 128), cw)] = gfin[...].astype(F32)
+    final.wait_recv()
+    gw_ref[:, pl.ds(pl.multiple_of((1 - c) * cw, 128), cw)] = gfull_in[...].astype(F32)
+    final.wait_send()
+
+    for i in range(2):
+        @pl.when(ups[i])
+        def _():
+            z_copy(i, everything, zup.at[i], zrecv.at[i, 0], up).wait_send()
+        y_copy(i, everything, yrecv.at[i, 0]).wait_send()
+        for j in range(2):
+            c_copy(i, j, everything).wait_send()
+
+    @pl.when(w == 1)
+    def _():
+        z_copy(1, everything, zdown.at[0], zrecv.at[1, 0], down).wait_send()
+    for t in range(2):
+        p_copy(t).wait_send()
+    for copy in sent:
+        copy.wait_send()
+
+
+def in_kernel(features, tiles, tile_cols, tile_mask, weight, bias, cotangent):
+    rows, width = features.shape
+    half = rows // 2
+    cw = width // 2
+    group_rows = width // 3
+    vmem = pl.BlockSpec(memory_space=pltpu.VMEM)
+    smem = pl.BlockSpec(memory_space=pltpu.SMEM)
+    hbm = pl.BlockSpec(memory_space=pl.ANY)
+    dma = pltpu.SemaphoreType.DMA
+    rbufs = [
+        pltpu.VMEM((WAYS[order[stage]] - 1, part_rows(group_rows, order, stage), cw), BF16)
+        for order in ORDERS
+        for stage in range(3)
+    ]
+    out, grad_weight, grad_bias = pl.pallas_call(
+        kernel,
+        out_shape=(
+            jax.ShapeDtypeStruct((half, width), BF16),
+            jax.ShapeDtypeStruct((width, width), F32),
+            jax.ShapeDtypeStruct((1, width), F32),
+        ),
+        in_specs=[hbm, hbm, smem, smem, hbm, vmem, hbm],
+        out_specs=(vmem, vmem, vmem),
+        scratch_shapes=[pltpu.VMEM((rows, width), BF16)] * 8
+        + [
+            pltpu.VMEM(tiles.shape, BF16),
+            pltpu.VMEM(weight.shape, BF16),
+            pltpu.VMEM(cotangent.shape, BF16),
+            pltpu.VMEM((8, rows, rows), BF16),
+            pltpu.VMEM((rows, width), F32),
+            pltpu.VMEM((half, width), BF16),
+            pltpu.VMEM((half, width), BF16),
+            pltpu.VMEM((half, width), BF16),
+            pltpu.VMEM((half, width), BF16),
+            pltpu.VMEM((width, cw), F32),
+            pltpu.VMEM((width, cw), BF16),
+            pltpu.VMEM((width, cw), BF16),
+            pltpu.VMEM((width, cw), BF16),
+            pltpu.VMEM((width, cw), BF16),
+            pltpu.VMEM((width, cw), BF16),
+        ]
+        + rbufs
+        + [
+            pltpu.VMEM((5, 8, width), F32),
+            pltpu.VMEM((6, 8, width), F32),
+            dma((4,)), dma((2, CHUNKS)), dma((2, CHUNKS)), dma((4,)),
+            dma((2,)), dma((1,)), dma((2,)), dma((4,)),
+            dma((2,)), dma((2,)), dma, dma,
+            dma((3, 3, 3)), dma((3, 3, 3)), dma((3, 3, 3)), dma((3, 3, 3)),
+            dma, dma, dma((6,)), dma((6,)),
+        ],
+        compiler_params=pltpu.CompilerParams(
+            collective_id=0, has_side_effects=True, vmem_limit_bytes=48 * 1024 * 1024
+        ),
+    )(features, tiles, tile_cols.reshape(-1), tile_mask.reshape(-1), weight, bias.reshape(1, -1), cotangent)
+    return out, grad_weight, grad_bias.reshape(-1)
+
+
 def solution(mesh):
     placed = (
         P("dom", None),
@@ -60,8 +465,9 @@
         P(),
         P(("dom", "rep"), None),
     )
+    body = in_kernel if (mesh.shape["dom"], mesh.shape["rep"]) == (16, 2) else on_device
     return jax.shard_map(
-        on_device,
+        body,
         mesh=mesh,
         in_specs=placed,
         out_specs=(P(("dom", "rep"), None), P(), P()),

time: 355 us -> 111 us (0.31)
  waiting for transfers between devices: 259 us -> 0 us
  Pallas kernels: 0 us -> 101 us
  blocking collectives: 39.6 us -> 0 us
  matrix products: 32 us -> 0 us
  between operations: 14 us -> 0.65 us
    psum x2 -> x0, waiting for transfers between devices: 242 us -> none  [the longest x1 144 us: spread(): return lax.psum(kept, axis)]
    pallas_call x0 -> x1, Pallas kernels: none -> 101 us  [in_kernel(): pl.pallas_call(kernel, out_shape=(jax.ShapeDtypeStruct((half, width), BF1...]
    psum x1 -> x0, blocking collectives: 39.6 us -> none  [on_device(): lax.psum((local_weight, local_bias), ('dom', 'rep'))]
    dot_general x18 -> x0, matrix products: 32 us -> none  [the longest x8 15.3 us: section_term(): jnp.einsum('bkij,bkjd->bid', tile_set, picked, preferred_element_type=jnp...]
    reduce_scatter x1 -> x0, waiting for transfers between devices: 17.6 us -> none  [on_device(): lax.psum_scatter(aggregate.astype(jnp.bfloat16), 'rep', scatter_dimension...]
    select_n x1 -> x0, other arithmetic: 3.97 us -> none  [spread(): jnp.where(lax.axis_index(axis) == source, value, 0).astype(value.dtype)]
    unnamed x27 -> x10, local copies, waits for them, and re-layouts: 3.91 us -> 7.13 us
  transfers between devices with their start and end apart: 3 -> 0, of which waited for: 3 -> 0; matrix products, arithmetic and copies ran while one was open for 0% -> 0% of each run, Pallas kernels for 0% -> 0%
where the time goes in v1:
time: 111 us
  Pallas kernels  101 us (91%)
  local copies, waits for them, and re-layouts  8.03 us (7%)
    pallas_call x1, Pallas kernels, in_kernel(): pl.pallas_call(kernel, out_shape=(jax.ShapeDtypeStruct((half, width), BF1...  101 us
    unnamed x10, local copies, waits for them, and re-layouts  7.13 us

profile of v1, /device:TPU:0, one launch (start us, length us, event | category | flops | bytes accessed | tf_op | source)
XLA Modules:
  0.0 110.7 jit_solution(10191620958305271313)
XLA Ops:
  0.6 0.8 copy.12
  1.4 0.1 reshape.18.cols
  1.5 0.8 copy.13
  2.3 0.1 reshape.19.mask
  2.4 0.7 reshape.20.bias_ref
  3.1 0.0 copy-start
  3.1 1.3 %copy-done = bf16[768,768]{1,0:T(8,128)(2,1)S(1)} copy-done((bf16[768,768]{1,0:T(8,128)(2,1)S(1)}, bf16[768,768]{1,0:T(8,128)(2,1)}, u32[]{:S(2)}) %copy-start) | copy-done | bytes 1179672
  4.4 0.0 copy-start.1
  4.4 1.1 %copy-done.1 = bf16[512,768]{1,0:T(8,128)(2,1)S(1)} copy-done((bf16[512,768]{1,0:T(8,128)(2,1)S(1)}, bf16[512,768]{1,0:T(8,128)(2,1)}, u32[]{:S(2)}) %copy-start.1) | copy-done | bytes 786456
  5.5 0.0 copy-start.2
  5.5 1.0 copy-done.2
  6.5 101.5 %shard_map.94 = (bf16[256,768]{1,0:T(8,128)(2,1)S(1)}, f32[768,768]{1,0:T(8,128)S(1)}, f32[1,768]{1,0:T(1,128)S(1)}) custom-call(bf16[512,768]{1,0:T(8,128)(2,1)S(1)} %copy-done.1, bf16[4,8,4,128,128]{4,3,2,1,0:T(8,128)(2,1)} %tiles_hbm.1, s32[128]{0:T(128)S(1)} %reshape.18.cols, s32[128]{0:T(128)S(1)} %reshape.19.mask, bf16[768,768]{1,0:T(8,128)(2,1)S(1)} %copy-done, ...), custom_call_target="tpu_custom_call" | custom-call | tf_op jit(solution)/shard_map/pallas_call | solution.py:414
  108.0 0.6 reduce
  108.6 0.7 copy.16
  109.3 1.4 %copy.17 = f32[768,768]{1,0:T(8,128)} copy(f32[768,768]{1,0:T(8,128)S(1)} %get-tuple-element.13) | data formatting | bytes 4718592
Async XLA Ops:
  3.1 1.3 %copy-start = (bf16[768,768]{1,0:T(8,128)(2,1)S(1)}, bf16[768,768]{1,0:T(8,128)(2,1)}, u32[]{:S(2)}) copy-start(bf16[768,768]{1,0:T(8,128)(2,1)} %weight_hbm.1) | copy-start | bytes 3538948
  4.4 1.1 %copy-start.1 = (bf16[512,768]{1,0:T(8,128)(2,1)S(1)}, bf16[512,768]{1,0:T(8,128)(2,1)}, u32[]{:S(2)}) copy-start(bf16[512,768]{1,0:T(8,128)(2,1)} %feat_hbm.1) | copy-start | bytes 2359300
  5.5 1.0 copy-start.2

commit v2 on v0

--- a/solution.py
+++ b/solution.py
@@ -1,7 +1,17 @@
+import functools
+
 import jax
 import jax.numpy as jnp
 from jax import lax
+from jax.experimental import pallas as pl
+from jax.experimental.pallas import tpu as pltpu
 from jax.sharding import PartitionSpec as P
+
+MESH = pl.DeviceIdType.MESH
+CHUNKS = 4
+THIRDS = 3
+F32 = jnp.float32
+BF16 = jnp.bfloat16
 
 
 def spread(value, axis, source):
@@ -50,6 +60,439 @@
     return (output, grad_weight, grad_bias)
 
 
+ORDERS = (("x", "y", "z"), ("y", "z", "x"), ("z", "x", "y"))
+WAYS = {"x": 2, "y": 2, "z": 4}
+
+
+def part_rows(group_rows, order, stage):
+    rows = group_rows
+    for axis in order[: stage + 1]:
+        rows //= WAYS[axis]
+    return rows
+
+
+def kernel(feat_hbm, tiles_hbm, cols, mask, weight_hbm, bias_ref, cot_hbm,
+           out_ref, gw_ref, gb_ref,
+           s000, s001, s010, s011, s100, s101, s110, s111,
+           tiles_v, weight_v, cot_v, dense, acc,
+           part_out, part_in, mixed, pre_acc, glow,
+           gacc, gsend, gcore_out, gcore_in, gfin, gfull_in,
+           rb00, rb01, rb02, rb10, rb11, rb12, rb20, rb21, rb22,
+           bstate, brecv,
+           lsem, zrecv, yrecv, crecv, zup, zdown, ysend, csend,
+           psend, precv, gcs, gcr, rs_s, rs_r, ag_s, ag_r, fs, fr, bs, br):
+    slots = [[[s000, s001], [s010, s011]], [[s100, s101], [s110, s111]]]
+    rbufs = [[rb00, rb01, rb02], [rb10, rb11, rb12], [rb20, rb21, rb22]]
+    me = lax.axis_index("dom")
+    r = lax.axis_index("rep")
+    z = lax.div(me, 4)
+    y = lax.rem(lax.div(me, 2), 2)
+    c = lax.rem(me, 2)
+    w = z + r * (3 - 2 * z)
+    dz = 1 - 2 * r
+    rblocks, sections, ways, side, _ = tiles_v.shape
+    _, rows, tw = acc.shape
+    width = THIRDS * tw
+    crows = rows // CHUNKS
+    half = rows // 2
+
+    def dev(zz, yy, cc, rr):
+        return (zz * 4 + yy * 2 + cc, rr)
+
+    def z_peer(d):
+        z2 = lax.rem(lax.div(z, 2) + d // 2, 2)
+        z1 = lax.rem(lax.rem(z, 2) + d % 2, 2)
+        return z2 * 2 + z1
+
+    peers = {
+        "x": [dev(z, y, c, 1 - r)],
+        "y": [dev(z, 1 - y, c, r)],
+        "z": [dev(z_peer(d), y, c, r) for d in (1, 2, 3)],
+    }
+    places = {"x": [1 - r], "y": [1 - y], "z": [z_peer(d) for d in (1, 2, 3)]}
+    mine = {"x": r, "y": y, "z": z}
+    other_core = dev(z, y, 1 - c, r)
+    up = dev(jnp.clip(z + dz, 0, 3), y, c, r)
+    down = dev(jnp.clip(z - dz, 0, 3), y, c, r)
+
+    def remote(src, dst, ss, rs, device):
+        return pltpu.make_async_remote_copy(
+            src_ref=src, dst_ref=dst, send_sem=ss, recv_sem=rs, device_id=device, device_id_type=MESH
+        )
+
+    def own_load(i, t):
+        return pltpu.make_async_copy(
+            feat_hbm.at[:, t * tw:(t + 1) * tw], slots[i][0][0].at[t], lsem.at[3 + t]
+        )
+
+    for i in range(2):
+        @pl.when(w == i)
+        def _():
+            for t in range(THIRDS):
+                own_load(i, t).start()
+    tiles_load = pltpu.make_async_copy(tiles_hbm, tiles_v, lsem.at[0])
+    weight_load = pltpu.make_async_copy(weight_hbm, weight_v, lsem.at[1])
+    cot_load = pltpu.make_async_copy(cot_hbm, cot_v, lsem.at[2])
+    tiles_load.start()
+    weight_load.start()
+    cot_load.start()
+    barrier = pltpu.get_barrier_semaphore()
+    greeted = [other_core] + peers["x"] + peers["y"] + peers["z"]
+    for device in greeted:
+        pl.semaphore_signal(barrier, inc=1, device_id=device, device_id_type=MESH)
+    pl.semaphore_wait(barrier, len(greeted))
+
+    everything = pl.ds(0, rows)
+
+    def chunk(ch):
+        return pl.ds(pl.multiple_of(ch * crows, crows), crows)
+
+    def z_copy(t, i, at, sem, rsem, device):
+        slot = slots[i][0][0]
+        return remote(slot.at[t, at], slot.at[t, at], sem, rsem, device)
+
+    def y_copy(t, i, at, rsem):
+        return remote(slots[i][0][0].at[t, at], slots[i][1][0].at[t, at],
+                      ysend.at[t, i], rsem, peers["y"][0])
+
+    def c_copy(t, i, j, at):
+        return remote(slots[i][j][0].at[t, at], slots[i][j][1].at[t, at],
+                      csend.at[t, 2 * i + j], crecv.at[t, 2 * i + j], other_core)
+
+    ups = {0: w <= 2, 1: jnp.logical_and(w >= 1, w <= 2)}
+
+    def forward(t, i, ch):
+        at = chunk(ch)
+
+        @pl.when(ups[i])
+        def _():
+            z_copy(t, i, at, zup.at[t, i], zrecv.at[t, i, ch], up).start()
+
+        if i == 1:
+            @pl.when(w == 1)
+            def _():
+                z_copy(t, i, at, zdown.at[t], zrecv.at[t, i, ch], down).start()
+        y_copy(t, i, at, yrecv.at[t, i, ch]).start()
+        c_copy(t, i, 0, at).start()
+
+    def up_sent(t, i):
+        z_copy(t, i, everything, zup.at[t, i], zrecv.at[t, i, 0], up).wait_send()
+
+    def own_step(t):
+        for i in range(2):
+            @pl.when(w == i)
+            def _():
+                own_load(i, t).wait()
+                if t > 0:
+                    up_sent(t - 1, i)
+
+                @pl.loop(0, CHUNKS)
+                def _(ch):
+                    forward(t, i, ch)
+
+    def z_step(t, i, ch):
+        @pl.when(w != i)
+        def _():
+            z_copy(t, i, chunk(ch), zup.at[t, i], zrecv.at[t, i, ch], up).wait_recv()
+            forward(t, i, ch)
+
+    def y_step(t, i, ch):
+        y_copy(t, i, chunk(ch), yrecv.at[t, i, ch]).wait_recv()
+        c_copy(t, i, 1, chunk(ch)).start()
+
+    def assemble(index):
+        i = 1 - lax.div(index, 4)
+        j = lax.rem(lax.div(index, 2), 2)
+        k = lax.rem(index, 2)
+        zz = i + r * (1 - 2 * i)
+        section = zz * 4 + (y + j - 2 * y * j) * 2 + (c + k - 2 * c * k)
+
+        @pl.loop(0, rblocks)
+        def _(b):
+            tile_of = [tiles_v[b, section, t].astype(F32) for t in range(ways)]
+            for block in range(rows // side):
+                total = None
+                for t in range(ways):
+                    take = jnp.logical_and(cols[b, t, section] == block, mask[b, t, section] != 0)
+                    term = tile_of[t] * jnp.where(take, 1.0, 0.0)
+                    total = term if total is None else total + term
+                dense[index, pl.ds(pl.multiple_of(b * side, side), side),
+                      block * side:(block + 1) * side] = total.astype(BF16)
+
+    def product(t, i, j, k, at):
+        index = (1 - i) * 4 + j * 2 + k
+        return jnp.dot(dense[index, at, :], slots[i][j][k][t], preferred_element_type=F32)
+
+    def add_product(t, i, j, k):
+        if k == 1:
+            c_copy(t, i, j, everything).wait_recv()
+        term = product(t, i, j, k, everything)
+        if (i, j, k) == (1, 0, 0):
+            acc[t] = term
+        else:
+            acc[t] = acc[t] + term
+
+    def p_copy(t):
+        return remote(part_out.at[t], part_in.at[t], psend.at[t], precv.at[t], peers["x"][0])
+
+    peer_rows = pl.ds(pl.multiple_of((1 - r) * half, half), half)
+    own_rows = pl.ds(pl.multiple_of(r * half, half), half)
+
+    def exchange(t):
+        part_out[t] = acc[t, peer_rows, :].astype(BF16)
+        p_copy(t).start()
+        mixed[t] = acc[t, own_rows, :].astype(BF16)
+
+    def meet(t):
+        p_copy(t).wait_recv()
+        low = (mixed[t].astype(F32) + part_in[t].astype(F32)).astype(BF16)
+        mixed[t] = low
+        return jnp.dot(low, weight_v[t * tw:(t + 1) * tw, :], preferred_element_type=F32)
+
+    jobs = [(i, j, k) for i in (1, 0) for j in range(2) for k in range(2)]
+    order = [(t, i, ch) for t in range(THIRDS) for i in (1, 0) for ch in range(CHUNKS)]
+    lag = 2
+    for position, (t, i, ch) in enumerate(order):
+        if i == 1 and ch == 0:
+            own_step(t)
+        if position == 0:
+            tiles_load.wait()
+        z_step(t, i, ch)
+        if position >= lag:
+            y_step(*order[position - lag])
+        step = position % (2 * CHUNKS)
+        if t == 0:
+            assemble(step)
+        elif t < THIRDS - 1:
+            add_product(t - 1, *jobs[step])
+            if step == 7:
+                exchange(t - 1)
+        elif step < 4:
+            add_product(t - 1, *jobs[2 * step])
+            add_product(t - 1, *jobs[2 * step + 1])
+            if step == 3:
+                exchange(t - 1)
+        else:
+            if step == 5:
+                weight_load.wait()
+                pre_acc[...] = meet(0) + bias_ref[...].reshape(1, width)
+            add_product(t, *jobs[step - 4])
+    for behind in range(lag, 0, -1):
+        y_step(*order[-behind])
+    last_third = THIRDS - 1
+    c_copy(last_third, 0, 0, everything).wait_recv()
+    c_copy(last_third, 0, 1, everything).wait_recv()
+
+    def finish(at, target):
+        total = acc[last_third, at, :]
+        for j in range(2):
+            for k in range(2):
+                total = total + product(last_third, 0, j, k, at)
+        target[last_third] = total.astype(BF16)
+
+    finish(peer_rows, part_out)
+    p_copy(last_third).start()
+    finish(own_rows, mixed)
+    for t in range(1, last_third):
+        pre_acc[...] = pre_acc[...] + meet(t)
+    cot_load.wait()
+    pre = pre_acc[...] + meet(last_third)
+    sig = 1.0 / (1.0 + jnp.exp(-pre))
+    out_ref[...] = (pre * sig).astype(BF16)
+    grad = cot_v[...].astype(F32) * sig * (1.0 + pre * (1.0 - sig))
+    glow[...] = grad.astype(BF16)
+    bias_rows = jnp.sum(grad.reshape(half // 8, 8, width), axis=0)
+
+    cw = width // 2
+    group_rows = tw
+
+    def grad_part(g, start):
+        lanes = pl.ds(pl.multiple_of(start, 128), cw)
+        return lax.dot_general(mixed[g], glow[:, lanes], (((0,), (0,)), ((), ())),
+                               preferred_element_type=F32)
+
+    def b_send(stage, axis_peers, first):
+        copies = []
+        for d, device in enumerate(axis_peers):
+            copies.append(remote(bstate.at[stage], brecv.at[first + d], bs.at[first + d],
+                                 br.at[first + d], device))
+            copies[-1].start()
+        return copies
+
+    def b_sum(stage, copies, first):
+        for copy in copies:
+            copy.wait_recv()
+        total = bstate[stage] + brecv[first]
+        if len(copies) == 3:
+            total = total + (brecv[first + 1] + brecv[first + 2])
+        bstate[stage + 1] = total
+
+    sent = []
+    bstate[0] = bias_rows
+    core_copies = []
+    for g in range(3):
+        at = pl.ds(g * group_rows, group_rows)
+        gcore_out[at, :] = grad_part(g, (1 - c) * cw).astype(BF16)
+        core_copies.append(remote(gcore_out.at[at], gcore_in.at[at], gcs.at[g], gcr.at[g], other_core))
+        core_copies[-1].start()
+    b_copies = b_send(0, [other_core], 0)
+    sent += core_copies + b_copies
+    for g in range(3):
+        gacc[pl.ds(g * group_rows, group_rows), :] = grad_part(g, c * cw)
+
+    starts = [g * group_rows for g in range(3)]
+    history = [[], [], []]
+    flying = [None, None, None]
+
+    def scatter(g, stage):
+        axis = ORDERS[g][stage]
+        size = part_rows(group_rows, ORDERS[g], stage)
+        copies = []
+        for d, (device, place) in enumerate(zip(peers[axis], places[axis])):
+            at = pl.ds(pl.multiple_of(starts[g] + place * size, size), size)
+            gsend[at, :] = gacc[at, :].astype(BF16)
+            copies.append(remote(gsend.at[at], rbufs[g][stage].at[d],
+                                 rs_s.at[g, stage, d], rs_r.at[g, stage, d], device))
+            copies[-1].start()
+        flying[g] = copies
+        sent.extend(copies)
+
+    def gather(g, stage):
+        axis = ORDERS[g][stage]
+        size = part_rows(group_rows, ORDERS[g], stage)
+        at = pl.ds(pl.multiple_of(starts[g], size), size)
+        arriving = []
+        for d, (device, place) in enumerate(zip(peers[axis], places[axis])):
+            copy = remote(gfin.at[at], gfin.at[at], ag_s.at[g, stage, d], ag_r.at[g, stage, d], device)
+            copy.start()
+            sent.append(copy)
+            there = pl.ds(pl.multiple_of(history[g][stage] + place * size, size), size)
+            arriving.append((there, remote(gfin.at[there], gfin.at[there], ag_s.at[g, stage, d],
+                                           ag_r.at[g, stage, d], device)))
+        starts[g] = history[g][stage]
+        flying[g] = arriving
+
+    def to_core(at):
+        remote(gfin.at[at], gfull_in.at[at], fs, fr, other_core).start()
+
+    for g in range(3):
+        at = pl.ds(g * group_rows, group_rows)
+        core_copies[g].wait_recv()
+        gacc[at, :] = gacc[at, :] + gcore_in[at, :].astype(F32)
+        scatter(g, 0)
+    b_sum(0, b_copies, 0)
+    b_first = (1, 2, 3)
+    for stage in range(3):
+        b_copies = b_send(stage + 1, peers[ORDERS[0][stage]], b_first[stage])
+        sent += b_copies
+        for g, order_g in enumerate(ORDERS):
+            size = part_rows(group_rows, order_g, stage)
+            for copy in flying[g]:
+                copy.wait_recv()
+            keep = starts[g] + mine[order_g[stage]] * size
+            at = pl.ds(pl.multiple_of(keep, size), size)
+            total = gacc[at, :]
+            for d in range(len(flying[g])):
+                total = total + rbufs[g][stage][d].astype(F32)
+            history[g].append(starts[g])
+            starts[g] = keep
+            if stage < 2:
+                gacc[at, :] = total
+                scatter(g, stage + 1)
+            else:
+                gfin[at, :] = total.astype(BF16)
+                gather(g, 2)
+                to_core(at)
+        b_sum(stage + 1, b_copies, b_first[stage])
+    for stage in (2, 1, 0):
+        for g in range(3):
+            arriving = flying[g]
+            for _, copy in arriving:
+                copy.wait_recv()
+            if stage > 0:
+                gather(g, stage - 1)
+            for there, _ in arriving:
+                to_core(there)
+    gb_ref[...] = jnp.sum(bstate[4], axis=0)
+    gw_ref[:, pl.ds(pl.multiple_of(c * cw, 128), cw)] = gfin[...].astype(F32)
+    final = remote(gfin, gfull_in, fs, fr, other_core)
+    final.wait_recv()
+    gw_ref[:, pl.ds(pl.multiple_of((1 - c) * cw, 128), cw)] = gfull_in[...].astype(F32)
+    final.wait_send()
+
+    for t in range(THIRDS):
+        for i in range(2):
+            waited = w != i if t < THIRDS - 1 else w >= 0
+
+            @pl.when(jnp.logical_and(ups[i], waited))
+            def _():
+                up_sent(t, i)
+            y_copy(t, i, everything, yrecv.at[t, i, 0]).wait_send()
+            for j in range(2):
+                c_copy(t, i, j, everything).wait_send()
+
+        @pl.when(w == 1)
+        def _():
+            z_copy(t, 1, everything, zdown.at[t], zrecv.at[t, 1, 0], down).wait_send()
+        p_copy(t).wait_send()
+    for copy in sent:
+        copy.wait_send()
+
+
+def in_kernel(features, tiles, tile_cols, tile_mask, weight, bias, cotangent):
+    rows, width = features.shape
+    half = rows // 2
+    cw = width // 2
+    tw = width // THIRDS
+    vmem = pl.BlockSpec(memory_space=pltpu.VMEM)
+    smem = pl.BlockSpec(memory_space=pltpu.SMEM)
+    hbm = pl.BlockSpec(memory_space=pltpu.HBM)
+    dma = pltpu.SemaphoreType.DMA
+    rbufs = [
+        pltpu.VMEM((WAYS[order[stage]] - 1, part_rows(tw, order, stage), cw), BF16)
+        for order in ORDERS
+        for stage in range(3)
+    ]
+    return pl.pallas_call(
+        kernel,
+        out_shape=(
+            jax.ShapeDtypeStruct((half, width), BF16),
+            jax.ShapeDtypeStruct((width, width), F32),
+            jax.ShapeDtypeStruct((width,), F32),
+        ),
+        in_specs=[hbm, hbm, smem, smem, hbm, vmem, hbm],
+        out_specs=(vmem, vmem, vmem),
+        scratch_shapes=[pltpu.VMEM((THIRDS, rows, tw), BF16)] * 8
+        + [
+            pltpu.VMEM(tiles.shape, BF16),
+            pltpu.VMEM(weight.shape, BF16),
+            pltpu.VMEM(cotangent.shape, BF16),
+            pltpu.VMEM((8, rows, rows), BF16),
+            pltpu.VMEM((THIRDS, rows, tw), F32),
+            pltpu.VMEM((THIRDS, half, tw), BF16),
+            pltpu.VMEM((THIRDS, half, tw), BF16),
+            pltpu.VMEM((THIRDS, half, tw), BF16),
+            pltpu.VMEM((half, width), F32),
+            pltpu.VMEM((half, width), BF16),
+            pltpu.VMEM((width, cw), F32),
+        ]
+        + [pltpu.VMEM((width, cw), BF16)] * 5
+        + rbufs
+        + [
+            pltpu.VMEM((5, 8, width), F32),
+            pltpu.VMEM((6, 8, width), F32),
+            dma((3 + THIRDS,)), dma((THIRDS, 2, CHUNKS)), dma((THIRDS, 2, CHUNKS)), dma((THIRDS, 4)),
+            dma((THIRDS, 2)), dma((THIRDS,)), dma((THIRDS, 2)), dma((THIRDS, 4)),
+            dma((THIRDS,)), dma((THIRDS,)), dma((3,)), dma((3,)),
+            dma((3, 3, 3)), dma((3, 3, 3)), dma((3, 3, 3)), dma((3, 3, 3)),
+            dma, dma, dma((6,)), dma((6,)),
+        ],
+        compiler_params=pltpu.CompilerParams(
+            collective_id=0, has_side_effects=True, vmem_limit_bytes=48 * 1024 * 1024
+        ),
+    )(features, tiles, tile_cols.transpose(0, 2, 1), tile_mask.transpose(0, 2, 1), weight, bias, cotangent)
+
+
 def solution(mesh):
     placed = (
         P("dom", None),
@@ -60,8 +503,9 @@
         P(),
         P(("dom", "rep"), None),
     )
+    body = in_kernel if (mesh.shape["dom"], mesh.shape["rep"]) == (16, 2) else on_device
     return jax.shard_map(
-        on_device,
+        body,
         mesh=mesh,
         in_specs=placed,
         out_specs=(P(("dom", "rep"), None), P(), P()),

time: 355 us -> 96.1 us (0.27)
  waiting for transfers between devices: 259 us -> 0 us
  Pallas kernels: 0 us -> 86.9 us
  blocking collectives: 39.6 us -> 0 us
  matrix products: 32 us -> 0 us
  between operations: 14 us -> 0.66 us
  other arithmetic: 3.97 us -> 0 us
    psum x2 -> x0, waiting for transfers between devices: 242 us -> none  [the longest x1 144 us: spread(): return lax.psum(kept, axis)]
    pallas_call x0 -> x1, Pallas kernels: none -> 86.9 us  [in_kernel(): pl.pallas_call(kernel, out_shape=(jax.ShapeDtypeStruct((half, width), BF1...]
    psum x1 -> x0, blocking collectives: 39.6 us -> none  [on_device(): lax.psum((local_weight, local_bias), ('dom', 'rep'))]
    dot_general x18 -> x0, matrix products: 32 us -> none  [the longest x8 15.3 us: section_term(): jnp.einsum('bkij,bkjd->bid', tile_set, picked, preferred_element_type=jnp...]
    reduce_scatter x1 -> x0, waiting for transfers between devices: 17.6 us -> none  [on_device(): lax.psum_scatter(aggregate.astype(jnp.bfloat16), 'rep', scatter_dimension...]
    unnamed x27 -> x15, local copies, waits for them, and re-layouts: 3.91 us -> 8.22 us
    select_n x1 -> x0, other arithmetic: 3.97 us -> none  [spread(): jnp.where(lax.axis_index(axis) == source, value, 0).astype(value.dtype)]
  transfers between devices with their start and end apart: 3 -> 0, of which waited for: 3 -> 0; matrix products, arithmetic and copies ran while one was open for 0% -> 0% of each run, Pallas kernels for 0% -> 0%
where the time goes in v2:
time: 96.1 us; the launch traced here: 95.7 us
  Pallas kernels  86.9 us (90%)
  local copies, waits for them, and re-layouts  8.22 us (9%)
    pallas_call x1, Pallas kernels, in_kernel(): pl.pallas_call(kernel, out_shape=(jax.ShapeDtypeStruct((half, width), BF1...  86.9 us
    unnamed x15, local copies, waits for them, and re-layouts  8.22 us

profile of v2, /device:TPU:0, one launch (start us, length us, event | category | flops | bytes accessed | tf_op | source)
XLA Modules:
  0.0 95.7 jit_solution(15271386736390884653)
XLA Ops:
  0.6 0.0 copy-start
  0.6 1.3 %copy-done = bf16[768,768]{1,0:T(8,128)(2,1)S(1)} copy-done((bf16[768,768]{1,0:T(8,128)(2,1)S(1)}, bf16[768,768]{1,0:T(8,128)(2,1)}, u32[]{:S(2)}) %copy-start) | copy-done | bytes 1179672
  1.9 0.0 copy-start.1
  1.9 1.1 %copy-done.1 = bf16[512,768]{1,0:T(8,128)(2,1)S(1)} copy-done((bf16[512,768]{1,0:T(8,128)(2,1)S(1)}, bf16[512,768]{1,0:T(8,128)(2,1)}, u32[]{:S(2)}) %copy-start.1) | copy-done | bytes 786456
  3.0 0.0 copy-start.2
  3.0 1.0 %copy-done.2 = bf16[256,768]{1,0:T(8,128)(2,1)S(1)} copy-done((bf16[256,768]{1,0:T(8,128)(2,1)S(1)}, bf16[256,768]{1,0:T(8,128)(2,1)}, u32[]{:S(2)}) %copy-start.2) | copy-done | bytes 393240
  4.0 0.0 copy-start.3
  4.0 0.7 copy-done.3
  4.7 0.0 copy-start.4
  4.7 0.7 copy-done.4
  5.4 0.0 copy-start.5
  5.4 0.7 copy-done.5
  6.1 86.9 %shard_map.94 = (bf16[256,768]{1,0:T(8,128)(2,1)S(1)}, f32[768,768]{1,0:T(8,128)S(1)}, f32[768]{0:T(1024)S(1)}) custom-call(bf16[512,768]{1,0:T(8,128)(2,1)S(1)} %copy-done.1, bf16[4,8,4,128,128]{4,3,2,1,0:T(8,128)(2,1)} %tiles_hbm.1, s32[4,4,8]{2,1,0:T(4,128)S(1)} %bitcast.2, s32[4,4,8]{2,1,0:T(4,128)S(1)} %bitcast.3, bf16[768,768]{1,0:T(8,128)(2,1)S(1)} %copy-done, ...), custom_call_target="tpu_custom_call" | custom-call | tf_op jit(solution)/shard_map/pallas_call | solution.py:456
  93.0 0.7 copy.13
  93.8 1.4 %copy.14 = f32[768,768]{1,0:T(8,128)} copy(f32[768,768]{1,0:T(8,128)S(1)} %get-tuple-element.7) | data formatting | bytes 4718592
  95.2 0.6 copy.15
Async XLA Ops:
  0.6 1.3 %copy-start = (bf16[768,768]{1,0:T(8,128)(2,1)S(1)}, bf16[768,768]{1,0:T(8,128)(2,1)}, u32[]{:S(2)}) copy-start(bf16[768,768]{1,0:T(8,128)(2,1)} %weight_hbm.1) | copy-start | bytes 3538948
  1.9 1.1 %copy-start.1 = (bf16[512,768]{1,0:T(8,128)(2,1)S(1)}, bf16[512,768]{1,0:T(8,128)(2,1)}, u32[]{:S(2)}) copy-start(bf16[512,768]{1,0:T(8,128)(2,1)} %feat_hbm.1) | copy-start | bytes 2359300
  3.0 1.0 %copy-start.2 = (bf16[256,768]{1,0:T(8,128)(2,1)S(1)}, bf16[256,768]{1,0:T(8,128)(2,1)}, u32[]{:S(2)}) copy-start(bf16[256,768]{1,0:T(8,128)(2,1)} %cot_hbm.1) | copy-start | bytes 1179652
  4.0 0.7 copy-start.3
  4.7 0.7 copy-start.4
  5.4 0.7 copy-start.5

commit v3 on v2

--- a/solution.py
+++ b/solution.py
@@ -71,12 +71,12 @@
     return rows
 
 
-def kernel(feat_hbm, tiles_hbm, cols, mask, weight_hbm, bias_ref, cot_hbm,
+def kernel(feat_hbm, tiles_hbm, cols_hbm, mask_hbm, weight_hbm, bias_hbm, cot_hbm,
            out_ref, gw_ref, gb_ref,
            s000, s001, s010, s011, s100, s101, s110, s111,
-           tiles_v, weight_v, cot_v, dense, acc,
-           part_out, part_in, mixed, pre_acc, glow,
-           gacc, gsend, gcore_out, gcore_in, gfin, gfull_in,
+           tiles_v, weight_v, cot_v, cols, mask, bias_ref, dense, acc,
+           part_out, part_in, mixed, mixed_t, pre_acc, glow,
+           gacc, gsend, gcore_out, gcore_in,
            rb00, rb01, rb02, rb10, rb11, rb12, rb20, rb21, rb22,
            bstate, brecv,
            lsem, zrecv, yrecv, crecv, zup, zdown, ysend, csend,
@@ -122,7 +122,7 @@
 
     def own_load(i, t):
         return pltpu.make_async_copy(
-            feat_hbm.at[:, t * tw:(t + 1) * tw], slots[i][0][0].at[t], lsem.at[3 + t]
+            feat_hbm.at[:, t * tw:(t + 1) * tw], slots[i][0][0].at[t], lsem.at[6 + t]
         )
 
     for i in range(2):
@@ -133,6 +133,12 @@
     tiles_load = pltpu.make_async_copy(tiles_hbm, tiles_v, lsem.at[0])
     weight_load = pltpu.make_async_copy(weight_hbm, weight_v, lsem.at[1])
     cot_load = pltpu.make_async_copy(cot_hbm, cot_v, lsem.at[2])
+    cols_load = pltpu.make_async_copy(cols_hbm, cols, lsem.at[3])
+    mask_load = pltpu.make_async_copy(mask_hbm, mask, lsem.at[4])
+    bias_load = pltpu.make_async_copy(bias_hbm, bias_ref, lsem.at[5])
+    cols_load.start()
+    mask_load.start()
+    bias_load.start()
     tiles_load.start()
     weight_load.start()
     cot_load.start()
@@ -256,6 +262,8 @@
         if i == 1 and ch == 0:
             own_step(t)
         if position == 0:
+            cols_load.wait()
+            mask_load.wait()
             tiles_load.wait()
         z_step(t, i, ch)
         if position >= lag:
@@ -275,11 +283,14 @@
         else:
             if step == 5:
                 weight_load.wait()
+                bias_load.wait()
                 pre_acc[...] = meet(0) + bias_ref[...].reshape(1, width)
             add_product(t, *jobs[step - 4])
     for behind in range(lag, 0, -1):
         y_step(*order[-behind])
     last_third = THIRDS - 1
+    for t in range(1, last_third):
+        pre_acc[...] = pre_acc[...] + meet(t)
     c_copy(last_third, 0, 0, everything).wait_recv()
     c_copy(last_third, 0, 1, everything).wait_recv()
 
@@ -293,10 +304,11 @@
     finish(peer_rows, part_out)
     p_copy(last_third).start()
     finish(own_rows, mixed)
-    for t in range(1, last_third):
-        pre_acc[...] = pre_acc[...] + meet(t)
+    for t in range(last_third):
+        mixed_t[t] = mixed[t].T
     cot_load.wait()
     pre = pre_acc[...] + meet(last_third)
+    mixed_t[last_third] = mixed[last_third].T
     sig = 1.0 / (1.0 + jnp.exp(-pre))
     out_ref[...] = (pre * sig).astype(BF16)
     grad = cot_v[...].astype(F32) * sig * (1.0 + pre * (1.0 - sig))
@@ -305,11 +317,12 @@
 
     cw = width // 2
     group_rows = tw
+    own_cols = pl.ds(pl.multiple_of(c * cw, 128), cw)
+    other_cols = pl.ds(pl.multiple_of((1 - c) * cw, 128), cw)
 
     def grad_part(g, start):
         lanes = pl.ds(pl.multiple_of(start, 128), cw)
-        return lax.dot_general(mixed[g], glow[:, lanes], (((0,), (0,)), ((), ())),
-                               preferred_element_type=F32)
+        return jnp.dot(mixed_t[g], glow[:, lanes], preferred_element_type=F32)
 
     def b_send(stage, axis_peers, first):
         copies = []
@@ -363,17 +376,17 @@
         at = pl.ds(pl.multiple_of(starts[g], size), size)
         arriving = []
         for d, (device, place) in enumerate(zip(peers[axis], places[axis])):
-            copy = remote(gfin.at[at], gfin.at[at], ag_s.at[g, stage, d], ag_r.at[g, stage, d], device)
+            copy = remote(gw_ref.at[at, own_cols], gw_ref.at[at, own_cols], ag_s.at[g, stage, d], ag_r.at[g, stage, d], device)
             copy.start()
             sent.append(copy)
             there = pl.ds(pl.multiple_of(history[g][stage] + place * size, size), size)
-            arriving.append((there, remote(gfin.at[there], gfin.at[there], ag_s.at[g, stage, d],
+            arriving.append((there, remote(gw_ref.at[there, own_cols], gw_ref.at[there, own_cols], ag_s.at[g, stage, d],
                                            ag_r.at[g, stage, d], device)))
         starts[g] = history[g][stage]
         flying[g] = arriving
 
     def to_core(at):
-        remote(gfin.at[at], gfull_in.at[at], fs, fr, other_core).start()
+        remote(gw_ref.at[at, own_cols], gw_ref.at[at, own_cols], fs, fr, other_core).start()
 
     for g in range(3):
         at = pl.ds(g * group_rows, group_rows)
@@ -400,7 +413,7 @@
                 gacc[at, :] = total
                 scatter(g, stage + 1)
             else:
-                gfin[at, :] = total.astype(BF16)
+                gw_ref[at, own_cols] = total.astype(BF16)
                 gather(g, 2)
                 to_core(at)
         b_sum(stage + 1, b_copies, b_first[stage])
@@ -414,11 +427,8 @@
             for there, _ in arriving:
                 to_core(there)
     gb_ref[...] = jnp.sum(bstate[4], axis=0)
-    gw_ref[:, pl.ds(pl.multiple_of(c * cw, 128), cw)] = gfin[...].astype(F32)
-    final = remote(gfin, gfull_in, fs, fr, other_core)
-    final.wait_recv()
-    gw_ref[:, pl.ds(pl.multiple_of((1 - c) * cw, 128), cw)] = gfull_in[...].astype(F32)
-    final.wait_send()
+    remote(gw_ref.at[:, other_cols], gw_ref.at[:, other_cols], fs, fr, other_core).wait_recv()
+    remote(gw_ref.at[:, own_cols], gw_ref.at[:, own_cols], fs, fr, other_core).wait_send()
 
     for t in range(THIRDS):
         for i in range(2):
@@ -445,7 +455,6 @@
     cw = width // 2
     tw = width // THIRDS
     vmem = pl.BlockSpec(memory_space=pltpu.VMEM)
-    smem = pl.BlockSpec(memory_space=pltpu.SMEM)
     hbm = pl.BlockSpec(memory_space=pltpu.HBM)
     dma = pltpu.SemaphoreType.DMA
     rbufs = [
@@ -453,44 +462,49 @@
         for order in ORDERS
         for stage in range(3)
     ]
-    return pl.pallas_call(
+    out, grad_weight, grad_bias = pl.pallas_call(
         kernel,
         out_shape=(
             jax.ShapeDtypeStruct((half, width), BF16),
-            jax.ShapeDtypeStruct((width, width), F32),
+            jax.ShapeDtypeStruct((width, width), BF16),
             jax.ShapeDtypeStruct((width,), F32),
         ),
-        in_specs=[hbm, hbm, smem, smem, hbm, vmem, hbm],
+        in_specs=[hbm] * 7,
         out_specs=(vmem, vmem, vmem),
         scratch_shapes=[pltpu.VMEM((THIRDS, rows, tw), BF16)] * 8
         + [
             pltpu.VMEM(tiles.shape, BF16),
             pltpu.VMEM(weight.shape, BF16),
             pltpu.VMEM(cotangent.shape, BF16),
+            pltpu.SMEM((tiles.shape[0], tiles.shape[2], tiles.shape[1]), jnp.int32),
+            pltpu.SMEM((tiles.shape[0], tiles.shape[2], tiles.shape[1]), jnp.int32),
+            pltpu.VMEM((width,), F32),
             pltpu.VMEM((8, rows, rows), BF16),
             pltpu.VMEM((THIRDS, rows, tw), F32),
             pltpu.VMEM((THIRDS, half, tw), BF16),
             pltpu.VMEM((THIRDS, half, tw), BF16),
             pltpu.VMEM((THIRDS, half, tw), BF16),
+            pltpu.VMEM((THIRDS, tw, half), BF16),
             pltpu.VMEM((half, width), F32),
             pltpu.VMEM((half, width), BF16),
             pltpu.VMEM((width, cw), F32),
         ]
-        + [pltpu.VMEM((width, cw), BF16)] * 5
+        + [pltpu.VMEM((width, cw), BF16)] * 3
         + rbufs
         + [
             pltpu.VMEM((5, 8, width), F32),
             pltpu.VMEM((6, 8, width), F32),
-            dma((3 + THIRDS,)), dma((THIRDS, 2, CHUNKS)), dma((THIRDS, 2, CHUNKS)), dma((THIRDS, 4)),
+            dma((6 + THIRDS,)), dma((THIRDS, 2, CHUNKS)), dma((THIRDS, 2, CHUNKS)), dma((THIRDS, 4)),
             dma((THIRDS, 2)), dma((THIRDS,)), dma((THIRDS, 2)), dma((THIRDS, 4)),
             dma((THIRDS,)), dma((THIRDS,)), dma((3,)), dma((3,)),
             dma((3, 3, 3)), dma((3, 3, 3)), dma((3, 3, 3)), dma((3, 3, 3)),
             dma, dma, dma((6,)), dma((6,)),
         ],
         compiler_params=pltpu.CompilerParams(
-            collective_id=0, has_side_effects=True, vmem_limit_bytes=48 * 1024 * 1024
+            collective_id=0, has_side_effects=True, vmem_limit_bytes=63 * 1024 * 1024
         ),
     )(features, tiles, tile_cols.transpose(0, 2, 1), tile_mask.transpose(0, 2, 1), weight, bias, cotangent)
+    return out, grad_weight.astype(F32), grad_bias
 
 
 def solution(mesh):

time: 96.1 us -> 92.7 us (0.965)
  local copies, waits for them, and re-layouts: 8.22 us -> 1.35 us
  other arithmetic: 0 us -> 2.89 us
    unnamed x15 -> x6, local copies, waits for them, and re-layouts: 8.22 us -> 1.35 us
    convert_element_type x0 -> x1, other arithmetic: none -> 2.89 us  [in_kernel(): return (out, grad_weight.astype(F32), grad_bias)]
where the time goes in v3:
time: 92.7 us; the launch traced here: 92.6 us
  Pallas kernels  87.7 us (95%)
  other arithmetic  2.89 us (3%)
  local copies, waits for them, and re-layouts  1.35 us (1%)
    pallas_call x1, Pallas kernels, in_kernel(): pl.pallas_call(kernel, out_shape=(jax.ShapeDtypeStruct((half, width), BF1...  87.7 us
    convert_element_type x1, other arithmetic, in_kernel(): return (out, grad_weight.astype(F32), grad_bias)  2.89 us

profile of v3, /device:TPU:0, one launch (start us, length us, event | category | flops | bytes accessed | tf_op | source)
XLA Modules:
  0.0 92.6 jit_solution(16052633600267182123)
XLA Ops:
  0.6 87.7 %shard_map.94 = (bf16[256,768]{1,0:T(8,128)(2,1)}, bf16[768,768]{1,0:T(8,128)(2,1)}, f32[768]{0:T(1024)}) custom-call(bf16[512,768]{1,0:T(8,128)(2,1)} %feat_hbm.1, bf16[4,8,4,128,128]{4,3,2,1,0:T(8,128)(2,1)} %tiles_hbm.1, s32[4,4,8]{2,1,0:T(4,128)} %bitcast.2, s32[4,4,8]{2,1,0:T(4,128)} %bitcast.3, bf16[768,768]{1,0:T(8,128)(2,1)} %weight_hbm.1, ...), custom_call_target="tpu_custom_call" | custom-call | tf_op jit(solution)/shard_map/pallas_call | solution.py:465
  88.3 0.0 copy-start
  88.3 0.0 copy-start.1
  88.3 2.9 %convert_element_type.3 = f32[768,768]{1,0:T(8,128)} convert(bf16[768,768]{1,0:T(8,128)(2,1)} %get-tuple-element.7) | non-fusion elementwise | flops 589824 | bytes 3538944 | tf_op jit(solution)/shard_map/convert_element_type | solution.py:507
  91.2 0.0 copy-done
  91.2 0.7 copy.12
  92.0 0.0 copy-done.1
  92.0 0.6 copy.13
Async XLA Ops:
  88.3 2.9 %copy-start = (bf16[256,768]{1,0:T(8,128)(2,1)S(1)}, bf16[256,768]{1,0:T(8,128)(2,1)}, u32[]{:S(2)}) copy-start(bf16[256,768]{1,0:T(8,128)(2,1)} %get-tuple-element.12) | copy-start | bytes 1179652
  88.3 3.7 %copy-start.1 = (f32[768]{0:T(1024)S(1)}, f32[768]{0:T(1024)}, u32[]{:S(2)}) copy-start(f32[768]{0:T(1024)} %get-tuple-element.14) | copy-start | bytes 9220

commit v4 on v3

--- a/solution.py
+++ b/solution.py
@@ -8,8 +8,9 @@
 from jax.sharding import PartitionSpec as P
 
 MESH = pl.DeviceIdType.MESH
-CHUNKS = 4
-THIRDS = 3
+UNITS = (3, 2, 1)
+CHUNKS = (8, 4, 4)
+PARTS = len(UNITS)
 F32 = jnp.float32
 BF16 = jnp.bfloat16
 
@@ -71,9 +72,15 @@
     return rows
 
 
+def column_parts(width):
+    unit = width // sum(UNITS)
+    wide = [u * unit for u in UNITS]
+    return [(sum(wide[:t]), wide[t]) for t in range(PARTS)]
+
+
 def kernel(feat_hbm, tiles_hbm, cols_hbm, mask_hbm, weight_hbm, bias_hbm, cot_hbm,
            out_ref, gw_ref, gb_ref,
-           s000, s001, s010, s011, s100, s101, s110, s111,
+           slots,
            tiles_v, weight_v, cot_v, cols, mask, bias_ref, dense, acc,
            part_out, part_in, mixed, mixed_t, pre_acc, glow,
            gacc, gsend, gcore_out, gcore_in,
@@ -81,7 +88,6 @@
            bstate, brecv,
            lsem, zrecv, yrecv, crecv, zup, zdown, ysend, csend,
            psend, precv, gcs, gcr, rs_s, rs_r, ag_s, ag_r, fs, fr, bs, br):
-    slots = [[[s000, s001], [s010, s011]], [[s100, s101], [s110, s111]]]
     rbufs = [[rb00, rb01, rb02], [rb10, rb11, rb12], [rb20, rb21, rb22]]
     me = lax.axis_index("dom")
     r = lax.axis_index("rep")
@@ -91,9 +97,8 @@
     w = z + r * (3 - 2 * z)
     dz = 1 - 2 * r
     rblocks, sections, ways, side, _ = tiles_v.shape
-    _, rows, tw = acc.shape
-    width = THIRDS * tw
-    crows = rows // CHUNKS
+    rows, width = feat_hbm.shape
+    parts = column_parts(width)
     half = rows // 2
 
     def dev(zz, yy, cc, rr):
@@ -122,13 +127,13 @@
 
     def own_load(i, t):
         return pltpu.make_async_copy(
-            feat_hbm.at[:, t * tw:(t + 1) * tw], slots[i][0][0].at[t], lsem.at[6 + t]
+            feat_hbm.at[:, pl.ds(*parts[t])], slots[i][0][0][t], lsem.at[6 + t]
         )
 
     for i in range(2):
         @pl.when(w == i)
         def _():
-            for t in range(THIRDS):
+            for t in range(PARTS):
                 own_load(i, t).start()
     tiles_load = pltpu.make_async_copy(tiles_hbm, tiles_v, lsem.at[0])
     weight_load = pltpu.make_async_copy(weight_hbm, weight_v, lsem.at[1])
@@ -150,25 +155,26 @@
 
     everything = pl.ds(0, rows)
 
-    def chunk(ch):
+    def chunk(t, ch):
+        crows = rows // CHUNKS[t]
         return pl.ds(pl.multiple_of(ch * crows, crows), crows)
 
     def z_copy(t, i, at, sem, rsem, device):
-        slot = slots[i][0][0]
-        return remote(slot.at[t, at], slot.at[t, at], sem, rsem, device)
+        slot = slots[i][0][0][t]
+        return remote(slot.at[at], slot.at[at], sem, rsem, device)
 
     def y_copy(t, i, at, rsem):
-        return remote(slots[i][0][0].at[t, at], slots[i][1][0].at[t, at],
+        return remote(slots[i][0][0][t].at[at], slots[i][1][0][t].at[at],
                       ysend.at[t, i], rsem, peers["y"][0])
 
     def c_copy(t, i, j, at):
-        return remote(slots[i][j][0].at[t, at], slots[i][j][1].at[t, at],
+        return remote(slots[i][j][0][t].at[at], slots[i][j][1][t].at[at],
                       csend.at[t, 2 * i + j], crecv.at[t, 2 * i + j], other_core)
 
     ups = {0: w <= 2, 1: jnp.logical_and(w >= 1, w <= 2)}
 
     def forward(t, i, ch):
-        at = chunk(ch)
+        at = chunk(t, ch)
 
         @pl.when(ups[i])
         def _():
@@ -192,19 +198,19 @@
                 if t > 0:
                     up_sent(t - 1, i)
 
-                @pl.loop(0, CHUNKS)
+                @pl.loop(0, CHUNKS[t])
                 def _(ch):
                     forward(t, i, ch)
 
     def z_step(t, i, ch):
         @pl.when(w != i)
         def _():
-            z_copy(t, i, chunk(ch), zup.at[t, i], zrecv.at[t, i, ch], up).wait_recv()
+            z_copy(t, i, chunk(t, ch), zup.at[t, i], zrecv.at[t, i, ch], up).wait_recv()
             forward(t, i, ch)
 
     def y_step(t, i, ch):
-        y_copy(t, i, chunk(ch), yrecv.at[t, i, ch]).wait_recv()
-        c_copy(t, i, 1, chunk(ch)).start()
+        y_copy(t, i, chunk(t, ch), yrecv.at[t, i, ch]).wait_recv()
+        c_copy(t, i, 1, chunk(t, ch)).start()
 
     def assemble(index):
         i = 1 - lax.div(index, 4)
@@ -227,36 +233,36 @@
 
     def product(t, i, j, k, at):
         index = (1 - i) * 4 + j * 2 + k
-        return jnp.dot(dense[index, at, :], slots[i][j][k][t], preferred_element_type=F32)
+        return jnp.dot(dense[index, at, :], slots[i][j][k][t][...], preferred_element_type=F32)
 
     def add_product(t, i, j, k):
         if k == 1:
             c_copy(t, i, j, everything).wait_recv()
         term = product(t, i, j, k, everything)
         if (i, j, k) == (1, 0, 0):
-            acc[t] = term
+            acc[t][...] = term
         else:
-            acc[t] = acc[t] + term
+            acc[t][...] = acc[t][...] + term
 
     def p_copy(t):
-        return remote(part_out.at[t], part_in.at[t], psend.at[t], precv.at[t], peers["x"][0])
+        return remote(part_out[t], part_in[t], psend.at[t], precv.at[t], peers["x"][0])
 
     peer_rows = pl.ds(pl.multiple_of((1 - r) * half, half), half)
     own_rows = pl.ds(pl.multiple_of(r * half, half), half)
 
     def exchange(t):
-        part_out[t] = acc[t, peer_rows, :].astype(BF16)
+        part_out[t][...] = acc[t][peer_rows, :].astype(BF16)
         p_copy(t).start()
-        mixed[t] = acc[t, own_rows, :].astype(BF16)
+        mixed[t][...] = acc[t][own_rows, :].astype(BF16)
 
     def meet(t):
         p_copy(t).wait_recv()
-        low = (mixed[t].astype(F32) + part_in[t].astype(F32)).astype(BF16)
-        mixed[t] = low
-        return jnp.dot(low, weight_v[t * tw:(t + 1) * tw, :], preferred_element_type=F32)
-
-    jobs = [(i, j, k) for i in (1, 0) for j in range(2) for k in range(2)]
-    order = [(t, i, ch) for t in range(THIRDS) for i in (1, 0) for ch in range(CHUNKS)]
+        low = (mixed[t][...].astype(F32) + part_in[t][...].astype(F32)).astype(BF16)
+        mixed[t][...] = low
+        return jnp.dot(low, weight_v[pl.ds(*parts[t]), :], preferred_element_type=F32)
+
+    jobs = [(j, k) for j in range(2) for k in range(2)]
+    order = [(t, i, ch) for t in range(PARTS) for i in (1, 0) for ch in range(CHUNKS[t])]
     lag = 2
     for position, (t, i, ch) in enumerate(order):
         if i == 1 and ch == 0:
@@ -268,47 +274,44 @@
         z_step(t, i, ch)
         if position >= lag:
             y_step(*order[position - lag])
-        step = position % (2 * CHUNKS)
-        if t == 0:
-            assemble(step)
-        elif t < THIRDS - 1:
-            add_product(t - 1, *jobs[step])
-            if step == 7:
-                exchange(t - 1)
-        elif step < 4:
-            add_product(t - 1, *jobs[2 * step])
-            add_product(t - 1, *jobs[2 * step + 1])
-            if step == 3:
-                exchange(t - 1)
-        else:
-            if step == 5:
-                weight_load.wait()
-                bias_load.wait()
-                pre_acc[...] = meet(0) + bias_ref[...].reshape(1, width)
-            add_product(t, *jobs[step - 4])
+        each = CHUNKS[t] // 4
+        turn = ch // each
+        if t == 0 and ch % each == 0:
+            assemble((1 - i) * 4 + turn)
+        if ch % each == each - 1:
+            if i == 0:
+                add_product(t, 1, *jobs[turn])
+            elif t > 0:
+                add_product(t - 1, 0, *jobs[turn])
+                if turn == 3:
+                    exchange(t - 1)
+        if (t, i, ch) == (PARTS - 1, 0, 0):
+            weight_load.wait()
+            bias_load.wait()
+            pre_acc[...] = meet(0) + bias_ref[...].reshape(1, width)
     for behind in range(lag, 0, -1):
         y_step(*order[-behind])
-    last_third = THIRDS - 1
-    for t in range(1, last_third):
+    last = PARTS - 1
+    for t in range(1, last):
         pre_acc[...] = pre_acc[...] + meet(t)
-    c_copy(last_third, 0, 0, everything).wait_recv()
-    c_copy(last_third, 0, 1, everything).wait_recv()
+    c_copy(last, 0, 0, everything).wait_recv()
+    c_copy(last, 0, 1, everything).wait_recv()
 
     def finish(at, target):
-        total = acc[last_third, at, :]
+        total = acc[last][at, :]
         for j in range(2):
             for k in range(2):
-                total = total + product(last_third, 0, j, k, at)
-        target[last_third] = total.astype(BF16)
+                total = total + product(last, 0, j, k, at)
+        target[last][...] = total.astype(BF16)
 
     finish(peer_rows, part_out)
-    p_copy(last_third).start()
+    p_copy(last).start()
     finish(own_rows, mixed)
-    for t in range(last_third):
-        mixed_t[t] = mixed[t].T
+    for t in range(last):
+        mixed_t[pl.ds(*parts[t]), :] = mixed[t][...].T
     cot_load.wait()
-    pre = pre_acc[...] + meet(last_third)
-    mixed_t[last_third] = mixed[last_third].T
+    pre = pre_acc[...] + meet(last)
+    mixed_t[pl.ds(*parts[last]), :] = mixed[last][...].T
     sig = 1.0 / (1.0 + jnp.exp(-pre))
     out_ref[...] = (pre * sig).astype(BF16)
     grad = cot_v[...].astype(F32) * sig * (1.0 + pre * (1.0 - sig))
@@ -316,13 +319,13 @@
     bias_rows = jnp.sum(grad.reshape(half // 8, 8, width), axis=0)
 
     cw = width // 2
-    group_rows = tw
+    group_rows = width // 3
     own_cols = pl.ds(pl.multiple_of(c * cw, 128), cw)
     other_cols = pl.ds(pl.multiple_of((1 - c) * cw, 128), cw)
 
     def grad_part(g, start):
         lanes = pl.ds(pl.multiple_of(start, 128), cw)
-        return jnp.dot(mixed_t[g], glow[:, lanes], preferred_element_type=F32)
+        return jnp.dot(mixed_t[pl.ds(g * group_rows, group_rows), :], glow[:, lanes], preferred_element_type=F32)
 
     def b_send(stage, axis_peers, first):
         copies = []
@@ -430,9 +433,9 @@
     remote(gw_ref.at[:, other_cols], gw_ref.at[:, other_cols], fs, fr, other_core).wait_recv()
     remote(gw_ref.at[:, own_cols], gw_ref.at[:, own_cols], fs, fr, other_core).wait_send()
 
-    for t in range(THIRDS):
+    for t in range(PARTS):
         for i in range(2):
-            waited = w != i if t < THIRDS - 1 else w >= 0
+            waited = w != i if t < PARTS - 1 else w >= 0
 
             @pl.when(jnp.logical_and(ups[i], waited))
             def _():
@@ -453,12 +456,17 @@
     rows, width = features.shape
     half = rows // 2
     cw = width // 2
-    tw = width // THIRDS
+    parts = column_parts(width)
     vmem = pl.BlockSpec(memory_space=pltpu.VMEM)
     hbm = pl.BlockSpec(memory_space=pltpu.HBM)
     dma = pltpu.SemaphoreType.DMA
+    most = max(CHUNKS)
+
+    def columns(height, dtype):
+        return [pltpu.VMEM((height, wide), dtype) for _, wide in parts]
+
     rbufs = [
-        pltpu.VMEM((WAYS[order[stage]] - 1, part_rows(tw, order, stage), cw), BF16)
+        pltpu.VMEM((WAYS[order[stage]] - 1, part_rows(width // 3, order, stage), cw), BF16)
         for order in ORDERS
         for stage in range(3)
     ]
@@ -471,8 +479,8 @@
         ),
         in_specs=[hbm] * 7,
         out_specs=(vmem, vmem, vmem),
-        scratch_shapes=[pltpu.VMEM((THIRDS, rows, tw), BF16)] * 8
-        + [
+        scratch_shapes=[
+            [[[columns(rows, BF16)] * 2] * 2] * 2,
             pltpu.VMEM(tiles.shape, BF16),
             pltpu.VMEM(weight.shape, BF16),
             pltpu.VMEM(cotangent.shape, BF16),
@@ -480,11 +488,11 @@
             pltpu.SMEM((tiles.shape[0], tiles.shape[2], tiles.shape[1]), jnp.int32),
             pltpu.VMEM((width,), F32),
             pltpu.VMEM((8, rows, rows), BF16),
-            pltpu.VMEM((THIRDS, rows, tw), F32),
-            pltpu.VMEM((THIRDS, half, tw), BF16),
-            pltpu.VMEM((THIRDS, half, tw), BF16),
-            pltpu.VMEM((THIRDS, half, tw), BF16),
-            pltpu.VMEM((THIRDS, tw, half), BF16),
+            columns(rows, F32),
+            columns(half, BF16),
+            columns(half, BF16),
+            columns(half, BF16),
+            pltpu.VMEM((width, half), BF16),
             pltpu.VMEM((half, width), F32),
             pltpu.VMEM((half, width), BF16),
             pltpu.VMEM((width, cw), F32),
@@ -494,9 +502,9 @@
         + [
             pltpu.VMEM((5, 8, width), F32),
             pltpu.VMEM((6, 8, width), F32),
-            dma((6 + THIRDS,)), dma((THIRDS, 2, CHUNKS)), dma((THIRDS, 2, CHUNKS)), dma((THIRDS, 4)),
-            dma((THIRDS, 2)), dma((THIRDS,)), dma((THIRDS, 2)), dma((THIRDS, 4)),
-            dma((THIRDS,)), dma((THIRDS,)), dma((3,)), dma((3,)),
+            dma((6 + PARTS,)), dma((PARTS, 2, most)), dma((PARTS, 2, most)), dma((PARTS, 4)),
+            dma((PARTS, 2)), dma((PARTS,)), dma((PARTS, 2)), dma((PARTS, 4)),
+            dma((PARTS,)), dma((PARTS,)), dma((3,)), dma((3,)),
             dma((3, 3, 3)), dma((3, 3, 3)), dma((3, 3, 3)), dma((3, 3, 3)),
             dma, dma, dma((6,)), dma((6,)),
         ],

time: 92.7 us -> 98.9 us (1.067)
  Pallas kernels: 87.7 us -> 93.8 us
    pallas_call x1, Pallas kernels: 87.7 us -> 93.8 us  [in_kernel(): pl.pallas_call(kernel, out_shape=(jax.ShapeDtypeStruct((half, width), BF1...]
where the time goes in v4:
time: 98.9 us; the launch traced here: 98.7 us
  Pallas kernels  93.8 us (95%)
  other arithmetic  2.89 us (3%)
  local copies, waits for them, and re-layouts  1.35 us (1%)
    pallas_call x1, Pallas kernels, in_kernel(): pl.pallas_call(kernel, out_shape=(jax.ShapeDtypeStruct((half, width), BF1...  93.8 us
    convert_element_type x1, other arithmetic, in_kernel(): return (out, grad_weight.astype(F32), grad_bias)  2.89 us

profile of v4, /device:TPU:0, one launch (start us, length us, event | category | flops | bytes accessed | tf_op | source)
XLA Modules:
  0.0 98.7 jit_solution(694713833815120890)
XLA Ops:
  0.6 93.8 %shard_map.94 = (bf16[256,768]{1,0:T(8,128)(2,1)}, bf16[768,768]{1,0:T(8,128)(2,1)}, f32[768]{0:T(1024)}) custom-call(bf16[512,768]{1,0:T(8,128)(2,1)} %feat_hbm.1, bf16[4,8,4,128,128]{4,3,2,1,0:T(8,128)(2,1)} %tiles_hbm.1, s32[4,4,8]{2,1,0:T(4,128)} %bitcast.2, s32[4,4,8]{2,1,0:T(4,128)} %bitcast.3, bf16[768,768]{1,0:T(8,128)(2,1)} %weight_hbm.1, ...), custom_call_target="tpu_custom_call" | custom-call | tf_op jit(solution)/shard_map/pallas_call | solution.py:473
  94.5 0.0 copy-start
  94.5 0.0 copy-start.1
  94.5 2.9 %convert_element_type.3 = f32[768,768]{1,0:T(8,128)} convert(bf16[768,768]{1,0:T(8,128)(2,1)} %get-tuple-element.7) | non-fusion elementwise | flops 589824 | bytes 3538944 | tf_op jit(solution)/shard_map/convert_element_type | solution.py:515
  97.4 0.0 copy-done
  97.4 0.7 copy.12
  98.1 0.0 copy-done.1
  98.1 0.6 copy.13
Async XLA Ops:
  94.5 2.9 %copy-start = (bf16[256,768]{1,0:T(8,128)(2,1)S(1)}, bf16[256,768]{1,0:T(8,128)(2,1)}, u32[]{:S(2)}) copy-start(bf16[256,768]{1,0:T(8,128)(2,1)} %get-tuple-element.12) | copy-start | bytes 1179652
  94.5 3.7 %copy-start.1 = (f32[768]{0:T(1024)S(1)}, f32[768]{0:T(1024)}, u32[]{:S(2)}) copy-start(f32[768]{0:T(1024)} %get-tuple-element.14) | copy-start | bytes 9220

commit v5 on v4

--- a/solution.py
+++ b/solution.py
@@ -8,8 +8,8 @@
 from jax.sharding import PartitionSpec as P
 
 MESH = pl.DeviceIdType.MESH
-UNITS = (3, 2, 1)
-CHUNKS = (8, 4, 4)
+UNITS = (2, 2, 2)
+CHUNKS = (4, 4, 4)
 PARTS = len(UNITS)
 F32 = jnp.float32
 BF16 = jnp.bfloat16
@@ -185,7 +185,6 @@
             def _():
                 z_copy(t, i, at, zdown.at[t], zrecv.at[t, i, ch], down).start()
         y_copy(t, i, at, yrecv.at[t, i, ch]).start()
-        c_copy(t, i, 0, at).start()
 
     def up_sent(t, i):
         z_copy(t, i, everything, zup.at[t, i], zrecv.at[t, i, 0], up).wait_send()
@@ -201,16 +200,20 @@
                 @pl.loop(0, CHUNKS[t])
                 def _(ch):
                     forward(t, i, ch)
+                c_copy(t, i, 0, everything).start()
 
     def z_step(t, i, ch):
         @pl.when(w != i)
         def _():
             z_copy(t, i, chunk(t, ch), zup.at[t, i], zrecv.at[t, i, ch], up).wait_recv()
             forward(t, i, ch)
+            if ch == CHUNKS[t] - 1:
+                c_copy(t, i, 0, everything).start()
 
     def y_step(t, i, ch):
         y_copy(t, i, chunk(t, ch), yrecv.at[t, i, ch]).wait_recv()
-        c_copy(t, i, 1, chunk(t, ch)).start()
+        if ch == CHUNKS[t] - 1:
+            c_copy(t, i, 1, everything).start()
 
     def assemble(index):
         i = 1 - lax.div(index, 4)

time: 98.9 us -> 95.9 us (0.970)
  Pallas kernels: 93.8 us -> 90.9 us
    pallas_call x1, Pallas kernels: 93.8 us -> 90.9 us  [in_kernel(): pl.pallas_call(kernel, out_shape=(jax.ShapeDtypeStruct((half, width), BF1...]
where the time goes in v5:
time: 95.9 us; the launch traced here: 95.8 us
  Pallas kernels  90.9 us (95%)
  other arithmetic  2.89 us (3%)
  local copies, waits for them, and re-layouts  1.35 us (1%)
    pallas_call x1, Pallas kernels, in_kernel(): pl.pallas_call(kernel, out_shape=(jax.ShapeDtypeStruct((half, width), BF1...  90.9 us
    convert_element_type x1, other arithmetic, in_kernel(): return (out, grad_weight.astype(F32), grad_bias)  2.89 us

profile of v5, /device:TPU:0, one launch (start us, length us, event | category | flops | bytes accessed | tf_op | source)
XLA Modules:
  0.0 95.8 jit_solution(9716707324528012703)
XLA Ops:
  0.6 90.9 %shard_map.94 = (bf16[256,768]{1,0:T(8,128)(2,1)}, bf16[768,768]{1,0:T(8,128)(2,1)}, f32[768]{0:T(1024)}) custom-call(bf16[512,768]{1,0:T(8,128)(2,1)} %feat_hbm.1, bf16[4,8,4,128,128]{4,3,2,1,0:T(8,128)(2,1)} %tiles_hbm.1, s32[4,4,8]{2,1,0:T(4,128)} %bitcast.2, s32[4,4,8]{2,1,0:T(4,128)} %bitcast.3, bf16[768,768]{1,0:T(8,128)(2,1)} %weight_hbm.1, ...), custom_call_target="tpu_custom_call" | custom-call | tf_op jit(solution)/shard_map/pallas_call | solution.py:476
  91.5 0.0 copy-start
  91.6 0.0 copy-start.1
  91.6 2.9 %convert_element_type.3 = f32[768,768]{1,0:T(8,128)} convert(bf16[768,768]{1,0:T(8,128)(2,1)} %get-tuple-element.7) | non-fusion elementwise | flops 589824 | bytes 3538944 | tf_op jit(solution)/shard_map/convert_element_type | solution.py:518
  94.5 0.0 copy-done
  94.5 0.7 copy.12
  95.2 0.0 copy-done.1
  95.2 0.6 copy.13
Async XLA Ops:
  91.5 2.9 %copy-start = (bf16[256,768]{1,0:T(8,128)(2,1)S(1)}, bf16[256,768]{1,0:T(8,128)(2,1)}, u32[]{:S(2)}) copy-start(bf16[256,768]{1,0:T(8,128)(2,1)} %get-tuple-element.12) | copy-start | bytes 1179652
  91.6 3.7 %copy-start.1 = (f32[768]{0:T(1024)S(1)}, f32[768]{0:T(1024)}, u32[]{:S(2)}) copy-start(f32[768]{0:T(1024)} %get-tuple-element.14) | copy-start | bytes 9220

commit v6 on v3

--- a/solution.py
+++ b/solution.py
@@ -257,7 +257,7 @@
 
     jobs = [(i, j, k) for i in (1, 0) for j in range(2) for k in range(2)]
     order = [(t, i, ch) for t in range(THIRDS) for i in (1, 0) for ch in range(CHUNKS)]
-    lag = 2
+    lag = 4
     for position, (t, i, ch) in enumerate(order):
         if i == 1 and ch == 0:
             own_step(t)
@@ -285,10 +285,13 @@
                 weight_load.wait()
                 bias_load.wait()
                 pre_acc[...] = meet(0) + bias_ref[...].reshape(1, width)
-            add_product(t, *jobs[step - 4])
+            if step > 5:
+                add_product(t, *jobs[step - 6])
+    last_third = THIRDS - 1
     for behind in range(lag, 0, -1):
         y_step(*order[-behind])
-    last_third = THIRDS - 1
+        if behind in (4, 3):
+            add_product(last_third, *jobs[6 - behind])
     for t in range(1, last_third):
         pre_acc[...] = pre_acc[...] + meet(t)
     c_copy(last_third, 0, 0, everything).wait_recv()

time: 92.7 us -> 89.5 us (0.965)
  Pallas kernels: 87.7 us -> 84.4 us
    pallas_call x1, Pallas kernels: 87.7 us -> 84.4 us  [in_kernel(): pl.pallas_call(kernel, out_shape=(jax.ShapeDtypeStruct((half, width), BF1...]
where the time goes in v6:
time: 89.5 us; the launch traced here: 89.3 us
  Pallas kernels  84.4 us (94%)
  other arithmetic  2.89 us (3%)
  local copies, waits for them, and re-layouts  1.35 us (2%)
    pallas_call x1, Pallas kernels, in_kernel(): pl.pallas_call(kernel, out_shape=(jax.ShapeDtypeStruct((half, width), BF1...  84.4 us
    convert_element_type x1, other arithmetic, in_kernel(): return (out, grad_weight.astype(F32), grad_bias)  2.89 us

profile of v6, /device:TPU:0, one launch (start us, length us, event | category | flops | bytes accessed | tf_op | source)
XLA Modules:
  0.0 89.3 jit_solution(11496351280196976238)
XLA Ops:
  0.6 84.4 %shard_map.94 = (bf16[256,768]{1,0:T(8,128)(2,1)}, bf16[768,768]{1,0:T(8,128)(2,1)}, f32[768]{0:T(1024)}) custom-call(bf16[512,768]{1,0:T(8,128)(2,1)} %feat_hbm.1, bf16[4,8,4,128,128]{4,3,2,1,0:T(8,128)(2,1)} %tiles_hbm.1, s32[4,4,8]{2,1,0:T(4,128)} %bitcast.2, s32[4,4,8]{2,1,0:T(4,128)} %bitcast.3, bf16[768,768]{1,0:T(8,128)(2,1)} %weight_hbm.1, ...), custom_call_target="tpu_custom_call" | custom-call | tf_op jit(solution)/shard_map/pallas_call | solution.py:468
  85.1 0.0 copy-start
  85.1 0.0 copy-start.1
  85.1 2.9 %convert_element_type.3 = f32[768,768]{1,0:T(8,128)} convert(bf16[768,768]{1,0:T(8,128)(2,1)} %get-tuple-element.7) | non-fusion elementwise | flops 589824 | bytes 3538944 | tf_op jit(solution)/shard_map/convert_element_type | solution.py:510
  88.0 0.0 copy-done
  88.0 0.7 copy.12
  88.7 0.0 copy-done.1
  88.7 0.6 copy.13
Async XLA Ops:
  85.1 2.9 %copy-start = (bf16[256,768]{1,0:T(8,128)(2,1)S(1)}, bf16[256,768]{1,0:T(8,128)(2,1)}, u32[]{:S(2)}) copy-start(bf16[256,768]{1,0:T(8,128)(2,1)} %get-tuple-element.12) | copy-start | bytes 1179652
  85.1 3.7 %copy-start.1 = (f32[768]{0:T(1024)S(1)}, f32[768]{0:T(1024)}, u32[]{:S(2)}) copy-start(f32[768]{0:T(1024)} %get-tuple-element.14) | copy-start | bytes 9220
